TPU v7x, 32 devices: a whole 2x2x4 slice. The times are simulated.
32 devices in a mesh: seq: 8 (over z, y), dp: 4 (over x, core).
Axes of the slice: x: 2, y: 2, z: 4, core: 2. Of those that a mesh axis runs over, the one named last changes fastest.
Arguments:
- inputs: float32 [4, 4096, 256], P('dp', 'seq'), may hold values from -6 to 6
- out_cotangent: float32 [4, 4096, 256], P('dp', 'seq'), may hold values from -6 to 6
- skip_cotangent: float32 [4, 4096, 256], P('dp', 'seq'), may hold values from -6 to 6
- convolution_weight: float32 [2, 512, 1024], replicated, may hold values from -0.25 to 0.25
- convolution_bias: float32 [2, 1024], replicated, may hold values from -3 to 3
- output_weight: float32 [2, 512, 512], replicated, may hold values from -0.25 to 0.25
Outputs:
- input_grad: float32 [4, 4096, 256], P('dp', 'seq')
- conv_grad: float32 [1024, 1024], P(('seq', 'dp'))
- out_grad: float32 [1024, 512], P(('seq', 'dp'))
- bias_grad: float32 [2048], P(('seq', 'dp'))
All inputs are finite; a program needn't handle non-finite values.
Results may differ from a plain program's by a relative error of at most 0.00025.
Values sent between devices are 32-bit elements; how exact they have to be, the bound alone decides.
A program may use at most 128 MiB of HBM per device.

v0:
```python
import math

import jax
import jax.numpy as jnp
from jax import lax
from jax.sharding import PartitionSpec as P


def from_behind(block, axis, distance):
    devices = range(lax.axis_size(axis))
    route = [(i - distance, i) for i in devices if i - distance in devices]
    return lax.ppermute(block, axis, route)


def matmul(left, right):
    return jnp.dot(left, right, precision=lax.Precision.HIGHEST, preferred_element_type=jnp.float32)


def contract(left, right, left_dim, right_dim):
    return lax.dot_general(
        left,
        right,
        (((left_dim,), (right_dim,)), ((), ())),
        precision=lax.Precision.HIGHEST,
        preferred_element_type=jnp.float32,
    )


def layer_forward_step(earlier, values, weight, bias):
    joined = jnp.concatenate([earlier, values], axis=1)
    mixed = matmul(joined, weight) + bias
    width = weight.shape[1] // 2
    tanh_part = jnp.tanh(mixed[:, :width])
    sigm_part = jax.nn.sigmoid(mixed[:, width:])
    return (joined, tanh_part, sigm_part, tanh_part * sigm_part)


def layer_backward_step(
    joined, tanh_part, sigm_part, hidden, weight, out_w, carried_state, skip_cotangent_rows
):
    channels = carried_state.shape[1]
    outer = jnp.concatenate([carried_state, skip_cotangent_rows], axis=1)
    dhidden = contract(outer, out_w, 1, 1)
    dfilter = dhidden * sigm_part * (1.0 - tanh_part * tanh_part)
    dgate = dhidden * tanh_part * sigm_part * (1.0 - sigm_part)
    dmixed = jnp.concatenate([dfilter, dgate], axis=1)
    out_t = contract(outer, hidden, 0, 0)
    conv_g = contract(joined, dmixed, 0, 0)
    bias_g = jnp.sum(dmixed, axis=0)
    back = contract(dmixed, weight, 1, 1)
    return (back[:, :channels], back[:, channels:], conv_g, out_t, bias_g)


def local(
    inputs, out_cotangent, skip_cotangent, convolution_weight, convolution_bias, output_weight
):
    start_row = inputs[0]
    output_cotangent_rows = out_cotangent[0]
    skip_cotangent_rows = skip_cotangent[0]
    rows, channels = start_row.shape
    half = rows // 2
    tail = from_behind(start_row[rows - half :], "seq", 1)
    earlier1 = jnp.concatenate([tail, start_row[: rows - half]], axis=0)
    first_joined, first_tanh, first_sigmoid, first_hidden = layer_forward_step(
        earlier1, start_row, convolution_weight[0], convolution_bias[0]
    )
    second_layer = start_row + matmul(first_hidden, output_weight[0][:, :channels])
    earlier2 = from_behind(second_layer, "seq", 1)
    second_joined, second_tanh, second_sigmoid, second_hidden = layer_forward_step(
        earlier2, second_layer, convolution_weight[1], convolution_bias[1]
    )
    past2, local2, second_conv_output, second_output, second_bias = layer_backward_step(
        second_joined,
        second_tanh,
        second_sigmoid,
        second_hidden,
        convolution_weight[1],
        output_weight[1],
        output_cotangent_rows,
        skip_cotangent_rows,
    )
    carried_state = output_cotangent_rows + local2 + from_behind(past2, "seq", -1)
    past1, local1, first_conv_output, first_output, first_bias = layer_backward_step(
        first_joined,
        first_tanh,
        first_sigmoid,
        first_hidden,
        convolution_weight[0],
        output_weight[0],
        carried_state,
        skip_cotangent_rows,
    )
    rim_rows = from_behind(past1[:half], "seq", -1)
    input_grad = carried_state + local1 + jnp.concatenate([past1[half:], rim_rows], axis=0)
    factor = 1.0 / math.sqrt(rows * lax.axis_size("seq") * lax.axis_size("dp"))
    conv_terms = jnp.concatenate([first_conv_output, second_conv_output], axis=0) * factor
    out_terms = jnp.concatenate([first_output, second_output], axis=0) * factor
    bias_terms = jnp.concatenate([first_bias, second_bias], axis=0) * factor
    conv_part, out_part, bias_part = (
        lax.psum_scatter(conv_terms, "seq", scatter_dimension=0, tiled=True),
        lax.psum_scatter(out_terms, "seq", scatter_dimension=0, tiled=True),
        lax.psum_scatter(bias_terms, "seq", scatter_dimension=0, tiled=True),
    )
    conv_grad, out_grad, bias_grad = (
        lax.psum_scatter(conv_part, "dp", scatter_dimension=0, tiled=True),
        lax.psum_scatter(out_part, "dp", scatter_dimension=0, tiled=True),
        lax.psum_scatter(bias_part, "dp", scatter_dimension=0, tiled=True),
    )
    return (input_grad[None], conv_grad, out_grad, bias_grad)


def solution(mesh):
    return jax.shard_map(
        local,
        mesh=mesh,
        in_specs=(P("dp", "seq", None), P("dp", "seq", None), P("dp", "seq", None), P(), P(), P()),
        out_specs=(
            P("dp", "seq", None),
            P(("seq", "dp"), None),
            P(("seq", "dp"), None),
            P(("seq", "dp")),
        ),
        check_vma=False,
    )
```

profile of v0, /device:TPU:0, one launch (start us, length us, event | category | flops | bytes accessed | tf_op | source)
XLA Modules:
  0.0 285.0 jit_solution(17718977691925044519)
XLA Ops:
  8.5 4.9 %collective-permute-start = (f32[256,256]{0,1:T(8,128)S(1)}, f32[256,256]{0,1:T(8,128)S(1)}, u32[]{:S(2)}, u32[]{:S(2)}) collective-permute-start(f32[256,256]{0,1:T(8,128)S(1)} %get-tuple-element.18), channel_id=1, source_target_pairs={{0,4},{4,8},{8,12},{12,16},{16,20},{20,24},{24,28},{1,5},{5,9},{9,... | collective-permute-start | bytes 786440 | tf_op jit(solution)/shard_map/ppermute | solution.py:12
  14.7 4.2 %collective-permute-done = f32[256,256]{0,1:T(8,128)S(1)} collective-permute-done((f32[256,256]{0,1:T(8,128)S(1)}, f32[256,256]{0,1:T(8,128)S(1)}, u32[]{:S(2)}, u32[]{:S(2)}) %collective-permute-start) | collective-permute-done | bytes 262176 | tf_op jit(solution)/shard_map/ppermute | solution.py:12
  18.9 5.3 %fusion.12 = f32[512,1024]{0,1:T(8,128)S(1)} fusion(f32[2,512,1024]{2,1,0:T(8,128)} %param.9, f32[1024]{0:T(1024)S(1)} %bitcast.48, f32[512,256]{0,1:T(8,128)S(1)} %bitcast.39, f32[256,256]{0,1:T(8,128)S(1)} %get-tuple-element.19, f32[256,256]{0,1:T(8,128)S(1)} %collective-permute-done), kind=kOutput, calls=%fused_computation.16 | convolution fusion | flops 3222274048 | bytes 5246976 | tf_op jit(solution)/shard_map/dot_general | solution.py:16
  25.7 4.6 %collective-permute-start.1 = (f32[512,256]{0,1:T(8,128)S(1)}, f32[512,256]{0,1:T(8,128)S(1)}, u32[]{:S(2)}, u32[]{:S(2)}) collective-permute-start(f32[512,256]{0,1:T(8,128)S(1)} %convolution_add_fusion), channel_id=1, source_target_pairs={{0,4},{4,8},{8,12},{12,16},{16,20},{20,24},{24,28},{1,5},{5,9},{9,... | collective-permute-start | bytes 1572872 | tf_op jit(solution)/shard_map/ppermute | solution.py:12
  31.3 2.0 copy.22
  33.3 7.0 %collective-permute-done.1 = f32[512,256]{0,1:T(8,128)S(1)} collective-permute-done((f32[512,256]{0,1:T(8,128)S(1)}, f32[512,256]{0,1:T(8,128)S(1)}, u32[]{:S(2)}, u32[]{:S(2)}) %collective-permute-start.1) | collective-permute-done | bytes 524320 | tf_op jit(solution)/shard_map/ppermute | solution.py:12
  40.4 5.3 %fusion.15 = f32[512,1024]{0,1:T(8,128)S(1)} fusion(f32[2,512,1024]{2,1,0:T(8,128)} %param.9, f32[1024]{0:T(1024)S(1)} %bitcast.47, f32[512,256]{0,1:T(8,128)S(1)} %convolution_add_fusion, f32[512,256]{0,1:T(8,128)S(1)} %collective-permute-done.1), kind=kOutput, calls=%fused_computation.17 | convolution fusion | flops 3222011904 | bytes 5246976 | tf_op jit(solution)/shard_map/dot_general | solution.py:16
  45.7 2.3 subtract_multiply_fusion.3
  48.0 3.6 %fusion = f32[512,512]{0,1:T(8,128)S(1)} fusion(f32[2,512,1024]{2,1,0:T(8,128)S(1)} %copy-done, f32[512,512]{0,1:T(8,128)S(1)} %get-tuple-element.15, f32[512,512]{0,1:T(8,128)S(1)} %get-tuple-element.14), kind=kOutput, calls=%fused_computation.4 | convolution fusion | flops 3221749760 | bytes 5242880 | tf_op jit(solution)/shard_map/dot_general | solution.py:20
  51.7 1.5 collective-permute-start.2
  53.2 2.1 fusion.30
  55.3 10.9 %collective-permute-done.2 = f32[512,256]{0,1:T(8,128)S(1)} collective-permute-done((f32[512,256]{0,1:T(8,128)S(1)}, f32[512,256]{0,1:T(8,128)S(1)}, u32[]{:S(2)}, u32[]{:S(2)}) %collective-permute-start.2) | collective-permute-done | bytes 524320 | tf_op jit(solution)/shard_map/ppermute | solution.py:12
  66.4 2.1 fusion.33
  68.5 1.6 maximum_multiply_fusion.1
  70.2 3.6 %fusion.21 = f32[512,1024]{1,0:T(8,128)S(1)} fusion(f32[512,512]{0,1:T(8,128)S(1)} %get-tuple-element.15, f32[512,512]{0,1:T(8,128)S(1)} %get-tuple-element.14, f32[512,256]{0,1:T(8,128)S(1)} %convolution_add_fusion, f32[512,256]{0,1:T(8,128)S(1)} %collective-permute-done.1), kind=kOutput, calls=%fused_computation.21 | convolution fusion | flops 3222011904 | bytes 5242880 | tf_op jit(solution)/shard_map/dot_general | solution.py:20
  73.9 2.3 subtract_multiply_fusion.1
  77.1 3.6 %fusion.19 = f32[512,1024]{1,0:T(8,128)S(1)} fusion(f32[512,512]{0,1:T(8,128)S(1)} %get-tuple-element.13, f32[512,512]{0,1:T(8,128)S(1)} %get-tuple-element.12, f32[512,256]{0,1:T(8,128)S(1)} %bitcast.40, f32[256,256]{0,1:T(8,128)S(1)} %get-tuple-element.19, f32[256,256]{0,1:T(8,128)S(1)} %copy-done.15), kind=kOutput, calls=%fused_computation.19 | convolution fusion | flops 3222274048 | bytes 5242880 | tf_op jit(solution)/shard_map/dot_general | solution.py:20
  80.7 2.5 maximum_multiply_fusion
  83.3 56.9 %reduce-scatter.9.cloned.1.call-done = f32[128,512]{1,0:T(8,128)} async-done(((f32[1024,512]{1,0:T(8,128)}), f32[128,512]{1,0:T(8,128)}) %reduce-scatter.9.cloned.1.call-update) | async-done | bytes 262160 | tf_op jit(solution)/shard_map/reduce_scatter | solution.py:101
  140.5 90.2 %reduce-scatter.5.cloned.1.call-done = f32[128,1024]{1,0:T(8,128)} async-done(((f32[1024,1024]{1,0:T(8,128)}), f32[128,1024]{1,0:T(8,128)}) %reduce-scatter.5.cloned.1.call-update) | async-done | bytes 524304 | tf_op jit(solution)/shard_map/reduce_scatter | solution.py:100
  230.8 5.4 %fusion.4 = f32[512,512]{0,1:T(8,128)S(1)} fusion(f32[2,512,1024]{2,1,0:T(8,128)} %param.9, f32[512,512]{0,1:T(8,128)} %copy-done.1, f32[512,512]{0,1:T(8,128)S(1)} %get-tuple-element.12), kind=kOutput, calls=%fused_computation.8 | convolution fusion | flops 3221749760 | bytes 5242880 | tf_op jit(solution)/shard_map/dot_general | solution.py:20
  243.2 22.4 %all-reduce = f32[2048]{0:T(1024)S(1)} all-reduce(f32[2048]{0:T(1024)S(1)} %maximum_multiply_fusion.2), channel_id=6, replica_groups=mesh['seq'=8,'dp'=4] {'seq'}, use_global_device_ids=true, to_apply=%region_6.0.clone | all-reduce | flops 2048 | bytes 16384
  265.8 5.6 %all-reduce.1 = f32[256]{0:T(256)S(1)} all-reduce(f32[256]{0:T(256)S(1)} %dynamic-slice.1), channel_id=7, replica_groups=mesh['seq'=8,'dp'=4] {'dp'}, use_global_device_ids=true, to_apply=%region_7.0.clone | all-reduce | flops 256 | bytes 2048
  274.1 4.3 %reduce-scatter.7.cloned.1.call-done = f32[32,1024]{1,0:T(8,128)} async-done(((f32[128,1024]{1,0:T(8,128)}), f32[32,1024]{1,0:T(8,128)}) %reduce-scatter.7.cloned.1.call-update) | async-done | bytes 131088 | tf_op jit(solution)/shard_map/reduce_scatter | solution.py:105
  (77 shorter events, 15.1 us)
Async XLA Ops:
  7.2 6.3 %copy-start.21 = (f32[2,1024]{1,0:T(2,128)S(1)}, f32[2,1024]{1,0:T(2,128)}, u32[]{:S(2)}) copy-start(f32[2,1024]{1,0:T(2,128)} %param.10) | copy-start | bytes 24580
  7.2 133.0 %reduce-scatter.9.cloned.1.call-start = ((), (), s32[]{:S(2)}) async-start(), calls=%async_computation.6 | async-start | bytes 2359296 | tf_op jit(solution)/shard_map/reduce_scatter | solution.py:101
  8.5 15.8 %copy-start.3 = (f32[1,512,256]{1,2,0:T(8,128)}, f32[1,512,256]{1,2,0:T(8,128)S(1)}, u32[]{:S(2)}) copy-start(f32[1,512,256]{1,2,0:T(8,128)S(1)} %copy.23) | copy-start | bytes 1572868
  8.5 10.4 %collective-permute-start = (f32[256,256]{0,1:T(8,128)S(1)}, f32[256,256]{0,1:T(8,128)S(1)}, u32[]{:S(2)}, u32[]{:S(2)}) collective-permute-start(f32[256,256]{0,1:T(8,128)S(1)} %get-tuple-element.18), channel_id=1, source_target_pairs={{0,4},{4,8},{8,12},{12,16},{16,20},{20,24},{24,28},{1,5},{5,9},{9,... | collective-permute-start | bytes 786440 | tf_op jit(solution)/shard_map/ppermute | solution.py:12
  18.9 5.3 %copy-start.14 = (f32[256,256]{0,1:T(8,128)}, f32[256,256]{0,1:T(8,128)S(1)}, u32[]{:S(2)}) copy-start(f32[256,256]{0,1:T(8,128)S(1)} %collective-permute-done) | copy-start | bytes 786436
  24.3 6.0 %copy-start.18 = (f32[1,512,256]{2,1,0:T(8,128)S(1)}, f32[1,512,256]{2,1,0:T(8,128)}, u32[]{:S(2)}) copy-start(f32[1,512,256]{2,1,0:T(8,128)} %param.7) | copy-start | bytes 1572868
  25.7 14.7 %collective-permute-start.1 = (f32[512,256]{0,1:T(8,128)S(1)}, f32[512,256]{0,1:T(8,128)S(1)}, u32[]{:S(2)}, u32[]{:S(2)}) collective-permute-start(f32[512,256]{0,1:T(8,128)S(1)} %convolution_add_fusion), channel_id=1, source_target_pairs={{0,4},{4,8},{8,12},{12,16},{16,20},{20,24},{24,28},{1,5},{5,9},{9,... | collective-permute-start | bytes 1572872 | tf_op jit(solution)/shard_map/ppermute | solution.py:12
  40.4 5.3 %copy-start.10 = (f32[1,512,256]{1,2,0:T(8,128)S(1)}, f32[1,512,256]{1,2,0:T(8,128)}, u32[]{:S(2)}) copy-start(f32[1,512,256]{1,2,0:T(8,128)} %copy.21) | copy-start | bytes 1572868
  40.4 5.4 %copy-start.16 = (f32[2,512,512]{2,1,0:T(8,128)S(1)}, f32[2,512,512]{2,1,0:T(8,128)}, u32[]{:S(2)}) copy-start(f32[2,512,512]{2,1,0:T(8,128)} %param.11) | copy-start | bytes 6291460
  40.4 5.4 %copy-start.19 = (f32[1,512,256]{1,2,0:T(8,128)S(1)}, f32[1,512,256]{1,2,0:T(8,128)}, u32[]{:S(2)}) copy-start(f32[1,512,256]{1,2,0:T(8,128)} %copy.22) | copy-start | bytes 1572868
  51.7 14.5 %collective-permute-start.2 = (f32[512,256]{0,1:T(8,128)S(1)}, f32[512,256]{0,1:T(8,128)S(1)}, u32[]{:S(2)}, u32[]{:S(2)}) collective-permute-start(f32[512,256]{0,1:T(8,128)S(1)} %slice.94), channel_id=1, source_target_pairs={{4,0},{8,4},{12,8},{16,12},{20,16},{24,20},{28,24},{5,1},{9,5},{13... | collective-permute-start | bytes 1572872 | tf_op jit(solution)/shard_map/ppermute | solution.py:12
  55.3 11.1 %copy-start.8 = (f32[512,1024]{0,1:T(8,128)S(1)}, f32[512,1024]{0,1:T(8,128)}, u32[]{:S(2)}) copy-start(f32[512,1024]{0,1:T(8,128)} %copy-done.7) | copy-start | bytes 6291460
  70.1 160.7 %reduce-scatter.5.cloned.1.call-start = ((), (), s32[]{:S(2)}) async-start(), calls=%async_computation.4 | async-start | bytes 4718592 | tf_op jit(solution)/shard_map/reduce_scatter | solution.py:100
  70.2 3.6 %copy-start.9 = (f32[512,1024]{0,1:T(8,128)S(1)}, f32[512,1024]{0,1:T(8,128)}, u32[]{:S(2)}) copy-start(f32[512,1024]{0,1:T(8,128)} %copy-done.7) | copy-start | bytes 6291460
  70.2 3.6 %copy-start.12 = (f32[512,256]{0,1:T(8,128)S(1)}, f32[512,256]{0,1:T(8,128)}, u32[]{:S(2)}) copy-start(f32[512,256]{0,1:T(8,128)} %copy-done.11) | copy-start | bytes 1572868
  70.2 3.6 %copy-start.17 = (f32[2,512,512]{2,1,0:T(8,128)S(1)}, f32[2,512,512]{2,1,0:T(8,128)}, u32[]{:S(2)}) copy-start(f32[2,512,512]{2,1,0:T(8,128)} %param.11) | copy-start | bytes 6291460
  70.2 3.6 %copy-start.20 = (f32[1,512,256]{1,2,0:T(8,128)S(1)}, f32[1,512,256]{1,2,0:T(8,128)}, u32[]{:S(2)}) copy-start(f32[1,512,256]{1,2,0:T(8,128)} %copy.22) | copy-start | bytes 1572868
  83.2 190.8 %reduce-scatter.11.cloned.1.call-start = ((), (), s32[]{:S(2)}) async-start(), calls=%async_computation.7 | async-start | bytes 327680 | tf_op jit(solution)/shard_map/reduce_scatter | solution.py:106
  140.2 138.2 %reduce-scatter.7.cloned.1.call-start = ((), (), s32[]{:S(2)}) async-start(), calls=%async_computation.5 | async-start | bytes 655360 | tf_op jit(solution)/shard_map/reduce_scatter | solution.py:105
  230.8 8.5 %copy-start.23 = (u32[32]{0:T(128)S(1)}, u32[32]{0:T(128)}, u32[]{:S(2)}) copy-start(u32[32]{0:T(128)} %constant.17) | copy-start | bytes 388
  230.8 9.1 %copy-start.22 = (u32[32]{0:T(128)S(1)}, u32[32]{0:T(128)}, u32[]{:S(2)}) copy-start(u32[32]{0:T(128)} %constant.13) | copy-start | bytes 388
  238.0 34.0 %collective-permute-start.3 = (f32[256,256]{0,1:T(8,128)}, f32[256,256]{0,1:T(8,128)}, u32[]{:S(2)}, u32[]{:S(2)}) collective-permute-start(f32[256,256]{0,1:T(8,128)} %get-tuple-element.17), channel_id=1, source_target_pairs={{4,0},{8,4},{12,8},{16,12},{20,16},{24,20},{28,24},{5,1},{9,5},{13... | collective-permute-start | bytes 786440 | tf_op jit(solution)/shard_map/ppermute | solution.py:12
  243.0 29.0 %copy-start.6 = (f32[512,512]{0,1:T(8,128)S(1)}, f32[512,512]{0,1:T(8,128)}, u32[]{:S(2)}) copy-start(f32[512,512]{0,1:T(8,128)} %copy-done.5) | copy-start | bytes 3145732
  243.0 29.0 %copy-start.13 = (f32[512,256]{0,1:T(8,128)S(1)}, f32[512,256]{0,1:T(8,128)}, u32[]{:S(2)}) copy-start(f32[512,256]{0,1:T(8,128)} %copy-done.11) | copy-start | bytes 1572868
  (8 other events, 15.6 us)
Sparse Core Ops, SparseCore 0:
  70.2 69.9 reduce-scatter.8
  143.8 86.8 reduce-scatter.4
  234.0 19.8 reduce-scatter.10
  256.7 21.6 reduce-scatter.6
where the time goes:
time: 285 us
  waiting for transfers between devices  174 us (61%)
  matrix products  36.9 us (13%)
  blocking collectives  28.1 us (10%)
  between operations  15.5 us (5%)
  starting transfers between devices  12.7 us (4%)
  local copies, waits for them, and re-layouts  12.3 us (4%)
  other arithmetic  5.78 us (2%)
    reduce_scatter x1, waiting for transfers between devices, local(): lax.psum_scatter(conv_terms, 'seq', scatter_dimension=0, tiled=True)  90.2 us
    reduce_scatter x1, waiting for transfers between devices, local(): lax.psum_scatter(out_terms, 'seq', scatter_dimension=0, tiled=True)  56.9 us
    unnamed x2, blocking collectives  28.1 us
    dot_general x8, matrix products, contract(): lax.dot_general(left, right, (((left_dim,), (right_dim,)), ((), ())), pre...  25 us
    ppermute x4, waiting for transfers between devices, from_behind(): return lax.ppermute(block, axis, route)  22.1 us
    ppermute x4, starting transfers between devices, from_behind(): return lax.ppermute(block, axis, route)  12.3 us
    dot_general x3, matrix products, matmul(): jnp.dot(left, right, precision=lax.Precision.HIGHEST, preferred_element_t...  12 us
    unnamed x56, local copies, waits for them, and re-layouts  10.2 us
  transfers between devices with their start and end apart: 8, of which 6 were waited for; matrix products, arithmetic and copies ran while one was open for 10% of the time, Pallas kernels for 0%

commit v1 on v0

v1 whole, which is shorter than its diff:
```python
import functools
import math

import jax
import jax.numpy as jnp
from jax import lax
from jax.experimental import pallas as pl
from jax.experimental.pallas import tpu as pltpu
from jax.sharding import PartitionSpec as P

F32, BF16 = jnp.float32, jnp.bfloat16
NN = (((1,), (0,)), ((), ()))
NT = (((1,), (1,)), ((), ()))
TILE = 256
X_FIRST = (896, 1152)


def split(value):
    high = value.astype(BF16)
    return high, (value - high.astype(F32)).astype(BF16)


def dot3(left, right, dims):
    product = functools.partial(lax.dot_general, dimension_numbers=dims, preferred_element_type=F32)
    (lh, ll), (rh, rl) = left, right
    return (product(ll, rh) + product(lh, rl)) + product(lh, rh)


def kernel(n_seq, n_dp, fused, factor, *refs):
    refs = list(refs)
    x, c2, sk, cw, cb, ow = refs[:6]
    ig, conv_o, out_o, bias_o = refs[6:10]
    (wch, wcl, woh, wol, jh, jl, jth, jtl, hh, hl, fa, ga, oth, otl, dhs, dzh, dzl,
     x2, x2p, tail, q2, q2r, q1, q1r, c1, bsum, ssem, rsem) = refs[10:38]
    if fused:
        grad, rc, rx, ry, rz = refs[38:]
    rows, chan = x.shape[1], x.shape[2]
    half = rows // 2
    gate = ow.shape[1]
    width = 3 * gate + 128
    A, B = pl.ds(0, half), pl.ds(half, half)

    seq, dp = lax.axis_index("seq"), lax.axis_index("dp")
    has_next, has_prev = seq < n_seq - 1, seq > 0
    nxt, prv = lax.rem(seq + 1, n_seq), lax.rem(seq + n_seq - 1, n_seq)
    me_z, me_y, me_x, me_c = seq // 2, seq % 2, dp // 2, dp % 2

    barrier = pltpu.get_barrier_semaphore()
    greet = [(nxt, dp), (prv, dp)]
    if fused:
        greet += [(seq, 2 * me_x + 1 - me_c), (seq, 2 * (1 - me_x) + me_c), (2 * me_z + 1 - me_y, dp)]
        greet += [(lax.rem(seq + 2 * k, n_seq), dp) for k in range(1, n_seq // 2)]
    for s, d in greet:
        pl.semaphore_signal(barrier, inc=1, device_id=(s, d), device_id_type=pl.DeviceIdType.MESH)
    pl.semaphore_wait(barrier, len(greet))

    def remote(src, dst, send, recv, s, d):
        return pltpu.make_async_remote_copy(
            src_ref=src, dst_ref=dst, send_sem=ssem.at[send], recv_sem=rsem.at[recv],
            device_id=(s, d), device_id_type=pl.DeviceIdType.MESH)

    t_copy = remote(x.at[0, B], tail, 0, 0, nxt, dp)
    x2_copy = [remote(x2.at[r], x2p.at[r], 1 + i, 1 + i, nxt, dp) for i, r in enumerate((A, B))]
    q2_copy = [remote(q2.at[r], q2r.at[r], 3 + i, 3 + i, prv, dp) for i, r in enumerate((A, B))]
    q1_copy = remote(q1.at[A], q1r, 5, 5, prv, dp)

    pl.when(has_next)(t_copy.start)

    @pl.when(jnp.logical_not(has_prev))
    def _():
        tail[...] = jnp.zeros_like(tail)
        x2p[...] = jnp.zeros_like(x2p)

    @pl.when(jnp.logical_not(has_next))
    def _():
        q2r[...] = jnp.zeros_like(q2r)
        q1r[...] = jnp.zeros_like(q1r)

    def split_weights(l):
        wch[l], wcl[l] = split(cw[l])
        woh[l], wol[l] = split(ow[l])

    def put_joined(l, r, c0, value):
        cols = pl.ds(c0, chan)
        jh[l, r, cols], jl[l, r, cols] = split(value)
        jth[l, cols, r], jtl[l, cols, r] = split(value.T)

    def put_outer(l, r, c0, value):
        cols = pl.ds(c0, chan)
        oth[l, cols, r], otl[l, cols, r] = split(value.T)

    def forward(l, r):
        joined = (jh[l, r, :], jl[l, r, :])
        for n in range(gate // TILE):
            cols, gcols = pl.ds(n * TILE, TILE), pl.ds(gate + n * TILE, TILE)
            f = dot3(joined, (wch[l, :, cols], wcl[l, :, cols]), NN) + cb[l:l + 1, cols]
            g = dot3(joined, (wch[l, :, gcols], wcl[l, :, gcols]), NN) + cb[l:l + 1, gcols]
            t, s = jnp.tanh(f), jax.nn.sigmoid(g)
            h = t * s
            fa[l, r, cols] = s * (1.0 - t * t)
            ga[l, r, cols] = h * (1.0 - s)
            hh[l, r, cols], hl[l, r, cols] = split(h)

    def second_input(r):
        out = pl.ds(0, chan)
        value = x[0, r, :] + dot3((hh[0, r, :], hl[0, r, :]), (woh[0, :, out], wol[0, :, out]), NN)
        x2[r, :] = value
        return value

    def dmixed(l, r, dh, i):
        df, dg = dh * fa[l, r, :], dh * ga[l, r, :]
        dzh[l, r, :gate], dzl[l, r, :gate] = split(df)
        dzh[l, r, gate:], dzl[l, r, gate:] = split(dg)
        bsum[l, i:i + 1, :gate] = jnp.sum(df, axis=0, keepdims=True)
        bsum[l, i:i + 1, gate:] = jnp.sum(dg, axis=0, keepdims=True)

    def back(l, r, c0):
        taps = pl.ds(c0, chan)
        return dot3((dzh[l, r, :], dzl[l, r, :]), (wch[l, taps, :], wcl[l, taps, :]), NT)

    def put_grad(l, kind, c0, value):
        if not fused:
            (conv_o if kind == 0 else out_o)[l, :, c0:c0 + TILE] = value
            return
        c0 += kind * 2 * gate
        block = value.shape[0] // 16
        for j in range(16):
            grad[l, j % 2, j // 2 % 2, j // 4 % 2, j // 8, :, c0:c0 + TILE] = value[j * block:(j + 1) * block]

    def out_grads(l):
        for n in range(gate // TILE):
            cols = pl.ds(n * TILE, TILE)
            put_grad(l, 1, n * TILE, dot3((oth[l], otl[l]), (hh[l, :, cols], hl[l, :, cols]), NN))

    def conv_grads(l):
        for n in range(2 * gate // TILE):
            cols = pl.ds(n * TILE, TILE)
            put_grad(l, 0, n * TILE, dot3((jth[l], jtl[l]), (dzh[l, :, cols], dzl[l, :, cols]), NN))
        total = bsum[l, 0:1, :] + bsum[l, 1:2, :]
        if not fused:
            bias_o[l:l + 1, :] = total
            return
        piece = 2 * gate // 16
        for j in range(16):
            spot = (l, j % 2, j // 2 % 2, j // 4 % 2, j // 8)
            grad[spot + (slice(None), slice(3 * gate, width))] = jnp.zeros((grad.shape[5], 128), F32)
            grad[spot + (slice(0, 1), slice(3 * gate, 3 * gate + piece))] = total[:, j * piece:(j + 1) * piece]

    copies = []

    def sums(l):
        base = 6 + 9 * l
        ax, by = pl.ds(0, X_FIRST[l]), pl.ds(X_FIRST[l], width - X_FIRST[l])
        other_c = (seq, 2 * me_x + 1 - me_c)
        other_x = (seq, 2 * (1 - me_x) + me_c)
        other_y = (2 * me_z + 1 - me_y, dp)
        own = grad.at[l, me_c]

        def go(src, dst, k, peer):
            copy = remote(src, dst, base + k, base + k, *peer)
            copy.start()
            copies.append(copy)
            return copy

        core = go(grad.at[l, 1 - me_c], rc.at[l], 0, other_c)
        yield
        core.wait_recv()
        own[...] += rc[l]
        xa = go(own.at[1 - me_x, :, :, :, ax], rx.at[l, :, :, :, ax], 1, other_x)
        yb = go(own.at[:, 1 - me_y, :, :, by], ry.at[l, :, :, :, by], 2, other_y)
        yield
        xa.wait_recv()
        own[me_x, :, :, :, ax] += rx[l, :, :, :, ax]
        ya = go(own.at[me_x, 1 - me_y, :, :, ax], ry.at[l, 0, :, :, ax], 3, other_y)
        yb.wait_recv()
        own[:, me_y, :, :, by] += ry[l, :, :, :, by]
        xb = go(own.at[1 - me_x, me_y, :, :, by], rx.at[l, 0, :, :, by], 4, other_x)
        yield
        ya.wait_recv()
        own[me_x, me_y, :, :, ax] += ry[l, 0, :, :, ax]
        xb.wait_recv()
        own[me_x, me_y, :, :, by] += rx[l, 0, :, :, by]
        to_owner = []
        for low in range(2):
            owner = 2 * l + low
            copy = remote(own.at[me_x, me_y, low], rz.at[l, me_z], base + 5 + low, base + 5 + me_z, 2 * owner + me_y, dp)
            pl.when(me_z != owner)(copy.start)
            to_owner.append((owner, copy))
        yield

        @pl.when(me_z // 2 == l)
        def _():
            rz[l, me_z] = own[me_x, me_y, me_z % 2]
            for z in range(4):
                landed = remote(rz.at[l, z], rz.at[l, z], base + 5, base + 5 + z, seq, dp)
                pl.when(me_z != z)(landed.wait_recv)
            total = ((rz[l, 0] + rz[l, 1]) + (rz[l, 2] + rz[l, 3])) * factor
            conv_o[...] = total[:, :2 * gate]
            out_o[...] = total[:, 2 * gate:3 * gate]
            bias_o[...] = total[:8, 3 * gate:]

        for owner, copy in to_owner:
            pl.when(me_z != owner)(copy.wait_send)
        yield

    split_weights(0)
    put_joined(0, B, 0, x[0, A, :])
    put_joined(0, A, chan, x[0, A, :])
    put_joined(0, B, chan, x[0, B, :])
    forward(0, B)
    second_b = second_input(B)
    pl.when(has_next)(x2_copy[1].start)
    put_joined(1, B, chan, second_b)
    split_weights(1)
    for r in (A, B):
        for l in range(2):
            put_outer(l, r, chan, sk[0, r, :])
        put_outer(1, r, 0, c2[0, r, :])
    late, early = pl.ds(chan, chan), pl.ds(0, chan)
    for r in (A, B):
        skip = split(sk[0, r, :])
        dhs[0, r, :] = dot3(skip, (woh[0, :, late], wol[0, :, late]), NT)
        dhs[1, r, :] = dot3(skip, (woh[1, :, late], wol[1, :, late]), NT) + dot3(
            split(c2[0, r, :]), (woh[1, :, early], wol[1, :, early]), NT)
    pl.when(has_prev)(t_copy.wait_recv)
    put_joined(0, A, 0, tail[...])
    forward(0, A)
    second_a = second_input(A)
    pl.when(has_next)(x2_copy[0].start)
    put_joined(1, A, chan, second_a)
    for i in (1, 0):
        r = (A, B)[i]
        pl.when(has_prev)(x2_copy[i].wait_recv)
        put_joined(1, r, 0, x2p[r, :])
        forward(1, r)
        dmixed(1, r, dhs[1, r, :], i)
        q2[r, :] = back(1, r, 0)
        pl.when(has_prev)(q2_copy[i].start)
    out_grads(1)
    conv_grads(1)
    if fused:
        second_sums = sums(1)
        next(second_sums)
    out_later = []
    for i in (1, 0):
        r = (A, B)[i]
        c1[r, :] = c2[0, r, :] + back(1, r, chan)
    if fused:
        next(second_sums)
    for i in (1, 0):
        r = (A, B)[i]
        pl.when(has_next)(q2_copy[i].wait_recv)
        carried = c1[r, :] + q2r[r, :]
        c1[r, :] = carried
        put_outer(0, r, 0, carried)
        dmixed(0, r, dhs[0, r, :] + dot3(split(carried), (woh[0, :, early], wol[0, :, early]), NT), i)
        q1[r, :] = back(0, r, 0)
        if i == 0:
            pl.when(has_prev)(q1_copy.start)
    out_grads(0)
    conv_grads(0)
    if fused:
        first_sums = sums(0)
        next(first_sums)
        next(second_sums)
    ig[0, A, :] = c1[A, :] + back(0, A, chan) + q1[B, :]
    if fused:
        next(first_sums)
    inner = c1[B, :] + back(0, B, chan)
    pl.when(has_next)(q1_copy.wait_recv)
    ig[0, B, :] = inner + q1r[...]
    if fused:
        next(second_sums)
        next(first_sums)
        next(first_sums)
        next(second_sums)
        next(first_sums)
    pl.when(has_next)(t_copy.wait_send)
    for i in range(2):
        pl.when(has_next)(x2_copy[i].wait_send)
        pl.when(has_prev)(q2_copy[i].wait_send)
    pl.when(has_prev)(q1_copy.wait_send)
    for copy in copies:
        copy.wait_send()


def local(n_seq, n_dp, *args):
    inputs, _, _, convolution_weight, _, output_weight = args
    _, rows, chan = inputs.shape
    half = rows // 2
    gate = output_weight.shape[1]
    fused = (n_seq, n_dp) == (8, 4)
    factor = 1.0 / math.sqrt(rows * n_seq * n_dp)
    block = 2 * (2 * chan) // (n_seq * n_dp)
    width = 3 * gate + 128
    vmem, sds = pltpu.VMEM, jax.ShapeDtypeStruct
    if fused:
        grads = [sds((block, 2 * gate), F32), sds((block, gate), F32), sds((8, 128), F32)]
    else:
        grads = [sds((2, 2 * chan, 2 * gate), F32), sds((2, 2 * chan, gate), F32), sds((2, 2 * gate), F32)]
    pair = lambda *shape: [vmem(shape, BF16)] * 2
    scratch = [
        *pair(2, 2 * chan, 2 * gate), *pair(2, gate, 2 * chan),
        *pair(2, rows, 2 * chan), *pair(2, 2 * chan, rows), *pair(2, rows, gate),
        vmem((2, rows, gate), F32), vmem((2, rows, gate), F32),
        *pair(2, 2 * chan, rows), vmem((2, rows, gate), F32), *pair(2, rows, 2 * gate),
        vmem((rows, chan), F32), vmem((rows, chan), F32), vmem((half, chan), F32),
        vmem((rows, chan), F32), vmem((rows, chan), F32), vmem((rows, chan), F32),
        vmem((half, chan), F32), vmem((rows, chan), F32), vmem((2, 8, 2 * gate), F32),
        pltpu.SemaphoreType.DMA((24,)), pltpu.SemaphoreType.DMA((24,)),
    ]
    if fused:
        scratch += [
            vmem((2, 2, 2, 2, 2, block, width), F32), vmem((2, 2, 2, 2, block, width), F32),
            vmem((2, 2, 2, block, width), F32), vmem((2, 2, 2, block, width), F32),
            vmem((2, 4, block, width), F32),
        ]
    spec = pl.BlockSpec(memory_space=pltpu.VMEM)
    input_grad, conv, out, bias = pl.pallas_call(
        functools.partial(kernel, n_seq, n_dp, fused, factor),
        out_shape=[sds(inputs.shape, F32)] + grads,
        in_specs=[spec] * 6,
        out_specs=[spec] * 4,
        scratch_shapes=scratch,
        compiler_params=pltpu.CompilerParams(
            collective_id=0, has_side_effects=True, vmem_limit_bytes=60 * 1024 * 1024),
    )(*args)
    if fused:
        return input_grad, conv, out, bias[0, : 4 * gate // (n_seq * n_dp)]

    def scattered(terms):
        terms = terms.reshape((-1,) + terms.shape[2:]) * factor
        part = lax.psum_scatter(terms, "seq", scatter_dimension=0, tiled=True)
        return lax.psum_scatter(part, "dp", scatter_dimension=0, tiled=True)

    return input_grad, scattered(conv), scattered(out), scattered(bias)


def solution(mesh):
    return jax.shard_map(
        functools.partial(local, mesh.shape["seq"], mesh.shape["dp"]),
        mesh=mesh,
        in_specs=(P("dp", "seq", None),) * 3 + (P(), P(), P()),
        out_specs=(P("dp", "seq", None), P(("seq", "dp"), None), P(("seq", "dp"), None), P(("seq", "dp"))),
        check_vma=False,
    )
```

time: 285 us -> 98.8 us (0.35)
  waiting for transfers between devices: 174 us -> 0 us
  Pallas kernels: 0 us -> 91.1 us
  matrix products: 36.9 us -> 0 us
  blocking collectives: 28.1 us -> 0 us
  between operations: 15.5 us -> 0.64 us
  starting transfers between devices: 12.7 us -> 0 us
  local copies, waits for them, and re-layouts: 12.3 us -> 6.1 us
  other arithmetic: 5.78 us -> 0 us
    reduce_scatter x4 -> x0, waiting for transfers between devices: 152 us -> none  [the longest x1 90.2 us: local(): lax.psum_scatter(conv_terms, 'seq', scatter_dimension=0, tiled=True)]
    pallas_call x0 -> x1, Pallas kernels: none -> 91.1 us  [local(): pl.pallas_call(functools.partial(kernel, n_seq, n_dp, fused, factor), out...]
    dot_general x11 -> x0, matrix products: 36.9 us -> none  [the longest x8 25 us: contract(): lax.dot_general(left, right, (((left_dim,), (right_dim,)), ((), ())), pre...]
    unnamed x2 -> x0, blocking collectives: 28.1 us -> none
    ppermute x4 -> x0, waiting for transfers between devices: 22.1 us -> none  [from_behind(): return lax.ppermute(block, axis, route)]
    ppermute x4 -> x0, starting transfers between devices: 12.3 us -> none  [from_behind(): return lax.ppermute(block, axis, route)]
    unnamed x56 -> x3, local copies, waits for them, and re-layouts: 10.2 us -> 4.91 us
    mul x3 -> x0, other arithmetic: 4.08 us -> none  [the longest x1 2.5 us: local(): jnp.concatenate([first_conv_output, second_conv_output], axis=0) * factor]
  transfers between devices with their start and end apart: 8 -> 0, of which waited for: 6 -> 0; matrix products, arithmetic and copies ran while one was open for 10% -> 0% of each run, Pallas kernels for 0% -> 0%
where the time goes in v1:
time: 98.8 us; the launch traced here: 97.8 us
  Pallas kernels  91.1 us (92%)
  local copies, waits for them, and re-layouts  6.1 us (6%)
    pallas_call x1, Pallas kernels, local(): pl.pallas_call(functools.partial(kernel, n_seq, n_dp, fused, factor), out...  91.1 us
    unnamed x3, local copies, waits for them, and re-layouts  4.91 us

profile of v1, /device:TPU:0, one launch (start us, length us, event | category | flops | bytes accessed | tf_op | source)
XLA Modules:
  0.0 97.8 jit_solution(18088520186768245180)
XLA Ops:
  0.6 91.1 %shard_map.93 = (f32[1,512,256]{2,1,0:T(8,128)}, f32[32,1024]{1,0:T(8,128)}, f32[32,512]{1,0:T(8,128)}, f32[8,128]{1,0:T(8,128)}) custom-call(f32[1,512,256]{2,1,0:T(8,128)} %refs_0_.1, f32[1,512,256]{2,1,0:T(8,128)} %refs_1_.1, f32[1,512,256]{2,1,0:T(8,128)} %refs_2_.1, f32[2,512,1024]{2,1,0:T(8,128)} %refs_3_.1, f32[2,1024]{1,0:T(2,128)} %refs_4_.1, ...), custom_call_target="tpu_custom_call" | custom-call | tf_op jit(solution)/shard_map/pallas_call | solution.py:319
  91.7 1.2 %slice_bitcast_fusion = f32[64]{0:T(128)} fusion(f32[8,128]{1,0:T(8,128)} %get-tuple-element.11), kind=kLoop, calls=%fused_computation | loop fusion | bytes 512 | tf_op jit(solution)/shard_map/squeeze | solution.py:329
  92.9 1.9 %copy.13 = f32[1,512,256]{2,1,0:T(8,128)} copy(f32[1,512,256]{2,1,0:T(8,128)} %get-tuple-element.16) | data formatting | bytes 1048576
  94.8 1.6 %copy.14 = f32[32,1024]{1,0:T(8,128)} copy(f32[32,1024]{1,0:T(8,128)} %get-tuple-element.17) | data formatting | bytes 262144
  96.3 1.5 %copy.15 = f32[32,512]{1,0:T(8,128)} copy(f32[32,512]{1,0:T(8,128)} %get-tuple-element.18) | data formatting | bytes 131072

commit v2 on v1

--- a/solution.py
+++ b/solution.py
@@ -12,7 +12,6 @@
 NN = (((1,), (0,)), ((), ()))
 NT = (((1,), (1,)), ((), ()))
 TILE = 256
-X_FIRST = (896, 1152)
 
 
 def split(value):
@@ -28,15 +27,15 @@
 
 def kernel(n_seq, n_dp, fused, factor, *refs):
     refs = list(refs)
-    x, c2, sk, cw, cb, ow = refs[:6]
+    x, c2_in, sk_in, cw_in, cb, ow_in = refs[:6]
     ig, conv_o, out_o, bias_o = refs[6:10]
     (wch, wcl, woh, wol, jh, jl, jth, jtl, hh, hl, fa, ga, oth, otl, dhs, dzh, dzl,
-     x2, x2p, tail, q2, q2r, q1, q1r, c1, bsum, ssem, rsem) = refs[10:38]
+     x2, x2p, tail, q2, q2r, q1, q1r, c1, bsum, c2, sk, cw, ow, ssem, rsem, lsem) = refs[10:43]
     if fused:
-        grad, rc, rx, ry, rz = refs[38:]
+        grad, rc, r1, r2, rz, rf = refs[43:]
     rows, chan = x.shape[1], x.shape[2]
     half = rows // 2
-    gate = ow.shape[1]
+    gate = ow_in.shape[1]
     width = 3 * gate + 128
     A, B = pl.ds(0, half), pl.ds(half, half)
 
@@ -44,6 +43,13 @@
     has_next, has_prev = seq < n_seq - 1, seq > 0
     nxt, prv = lax.rem(seq + 1, n_seq), lax.rem(seq + n_seq - 1, n_seq)
     me_z, me_y, me_x, me_c = seq // 2, seq % 2, dp // 2, dp % 2
+
+    fetches = {}
+    for i, (name, src, dst) in enumerate((
+        ("cw0", cw_in.at[0], cw.at[0]), ("ow0", ow_in.at[0], ow.at[0]), ("sk", sk_in, sk),
+        ("c2", c2_in, c2), ("ow1", ow_in.at[1], ow.at[1]), ("cw1", cw_in.at[1], cw.at[1]))):
+        fetches[name] = pltpu.make_async_copy(src, dst, lsem.at[i])
+        fetches[name].start()
 
     barrier = pltpu.get_barrier_semaphore()
     greet = [(nxt, dp), (prv, dp)]
@@ -76,8 +82,12 @@
         q2r[...] = jnp.zeros_like(q2r)
         q1r[...] = jnp.zeros_like(q1r)
 
-    def split_weights(l):
+    def split_conv(l):
+        fetches["cw%d" % l].wait()
         wch[l], wcl[l] = split(cw[l])
+
+    def split_out(l):
+        fetches["ow%d" % l].wait()
         woh[l], wol[l] = split(ow[l])
 
     def put_joined(l, r, c0, value):
@@ -127,15 +137,16 @@
         for j in range(16):
             grad[l, j % 2, j // 2 % 2, j // 4 % 2, j // 8, :, c0:c0 + TILE] = value[j * block:(j + 1) * block]
 
-    def out_grads(l):
-        for n in range(gate // TILE):
-            cols = pl.ds(n * TILE, TILE)
-            put_grad(l, 1, n * TILE, dot3((oth[l], otl[l]), (hh[l, :, cols], hl[l, :, cols]), NN))
-
-    def conv_grads(l):
-        for n in range(2 * gate // TILE):
-            cols = pl.ds(n * TILE, TILE)
-            put_grad(l, 0, n * TILE, dot3((jth[l], jtl[l]), (dzh[l, :, cols], dzl[l, :, cols]), NN))
+    def grad_tile(l, k):
+        if k < n_out:
+            cols = pl.ds(k * TILE, TILE)
+            put_grad(l, 1, k * TILE, dot3((oth[l], otl[l]), (hh[l, :, cols], hl[l, :, cols]), NN))
+            return
+        c0 = (k - n_out) * TILE
+        cols = pl.ds(c0, TILE)
+        put_grad(l, 0, c0, dot3((jth[l], jtl[l]), (dzh[l, :, cols], dzl[l, :, cols]), NN))
+
+    def bias_grad(l):
         total = bsum[l, 0:1, :] + bsum[l, 1:2, :]
         if not fused:
             bias_o[l:l + 1, :] = total
@@ -146,88 +157,143 @@
             grad[spot + (slice(None), slice(3 * gate, width))] = jnp.zeros((grad.shape[5], 128), F32)
             grad[spot + (slice(0, 1), slice(3 * gate, 3 * gate + piece))] = total[:, j * piece:(j + 1) * piece]
 
+    n_out, tiles = gate // TILE, 3 * gate // TILE
     copies = []
 
-    def sums(l):
-        base = 6 + 9 * l
-        ax, by = pl.ds(0, X_FIRST[l]), pl.ds(X_FIRST[l], width - X_FIRST[l])
+    def go(src, dst, k, peer):
+        copy = remote(src, dst, k, k, *peer)
+        copy.start()
+        copies.append(copy)
+        return copy
+
+    def chunk(l, k):
+        base = 6 + 6 * (tiles * l + k)
+        if k < n_out:
+            c0, size = 2 * gate + k * TILE, TILE
+        else:
+            c0, size = (k - n_out) * TILE, TILE
+        if k == n_out - 1:
+            size += 128
+        cols = pl.ds(c0, size)
+        x_first = k % 2 == 0
         other_c = (seq, 2 * me_x + 1 - me_c)
         other_x = (seq, 2 * (1 - me_x) + me_c)
         other_y = (2 * me_z + 1 - me_y, dp)
         own = grad.at[l, me_c]
-
-        def go(src, dst, k, peer):
-            copy = remote(src, dst, base + k, base + k, *peer)
-            copy.start()
-            copies.append(copy)
-            return copy
-
-        core = go(grad.at[l, 1 - me_c], rc.at[l], 0, other_c)
+        place = me_z if l == 0 else 3 - me_z
+        low = lambda p: p if l == 0 else 1 - p
+        at_place = lambda p: (2 * (p if l == 0 else 3 - p) + me_y, dp)
+
+        if k == n_out - 1:
+            bias_grad(l)
+        grad_tile(l, k)
+        core = go(grad.at[l, 1 - me_c, :, :, :, :, cols], rc.at[l, :, :, :, :, cols], base, other_c)
         yield
         core.wait_recv()
-        own[...] += rc[l]
-        xa = go(own.at[1 - me_x, :, :, :, ax], rx.at[l, :, :, :, ax], 1, other_x)
-        yb = go(own.at[:, 1 - me_y, :, :, by], ry.at[l, :, :, :, by], 2, other_y)
-        yield
-        xa.wait_recv()
-        own[me_x, :, :, :, ax] += rx[l, :, :, :, ax]
-        ya = go(own.at[me_x, 1 - me_y, :, :, ax], ry.at[l, 0, :, :, ax], 3, other_y)
-        yb.wait_recv()
-        own[:, me_y, :, :, by] += ry[l, :, :, :, by]
-        xb = go(own.at[1 - me_x, me_y, :, :, by], rx.at[l, 0, :, :, by], 4, other_x)
-        yield
-        ya.wait_recv()
-        own[me_x, me_y, :, :, ax] += ry[l, 0, :, :, ax]
-        xb.wait_recv()
-        own[me_x, me_y, :, :, by] += rx[l, 0, :, :, by]
-        to_owner = []
-        for low in range(2):
-            owner = 2 * l + low
-            copy = remote(own.at[me_x, me_y, low], rz.at[l, me_z], base + 5 + low, base + 5 + me_z, 2 * owner + me_y, dp)
-            pl.when(me_z != owner)(copy.start)
-            to_owner.append((owner, copy))
-        yield
-
-        @pl.when(me_z // 2 == l)
+        own[:, :, :, :, cols] += rc[l, :, :, :, :, cols]
+        if x_first:
+            first = go(own.at[1 - me_x, :, :, :, cols], r1.at[l, :, :, :, cols], base + 1, other_x)
+        else:
+            first = go(own.at[:, 1 - me_y, :, :, cols], r1.at[l, :, :, :, cols], base + 1, other_y)
+        yield
+        first.wait_recv()
+        if x_first:
+            own[me_x, :, :, :, cols] += r1[l, :, :, :, cols]
+            second = go(own.at[me_x, 1 - me_y, :, :, cols], r2.at[l, :, :, cols], base + 2, other_y)
+        else:
+            own[:, me_y, :, :, cols] += r1[l, :, :, :, cols]
+            second = go(own.at[1 - me_x, me_y, :, :, cols], r2.at[l, :, :, cols], base + 2, other_x)
+        yield
+        second.wait_recv()
+        mine = own.at[me_x, me_y]
+        mine[:, :, cols] += r2[l, :, :, cols]
+        both = [remote(mine.at[:, :, cols], rz.at[l, :, :, cols], base + 3, base + 3, *at_place(p)) for p in (1, 2)]
+        up = remote(mine.at[low(0), :, cols], rf.at[l, :, cols], base + 3, base + 4, *at_place(0))
+        down = remote(mine.at[low(1), :, cols], rf.at[l, :, cols], base + 3, base + 4, *at_place(1))
+        pl.when(place == 3)(both[1].start)
+        pl.when(place == 0)(down.start)
+        yield
+
+        @pl.when(place == 2)
         def _():
-            rz[l, me_z] = own[me_x, me_y, me_z % 2]
-            for z in range(4):
-                landed = remote(rz.at[l, z], rz.at[l, z], base + 5, base + 5 + z, seq, dp)
-                pl.when(me_z != z)(landed.wait_recv)
-            total = ((rz[l, 0] + rz[l, 1]) + (rz[l, 2] + rz[l, 3])) * factor
-            conv_o[...] = total[:, :2 * gate]
-            out_o[...] = total[:, 2 * gate:3 * gate]
-            bias_o[...] = total[:8, 3 * gate:]
-
-        for owner, copy in to_owner:
-            pl.when(me_z != owner)(copy.wait_send)
-        yield
-
-    split_weights(0)
+            both[1].wait_recv()
+            mine[:, :, cols] += rz[l, :, :, cols]
+            both[0].start()
+
+        yield
+
+        def finish(p):
+            total = (mine[low(p), :, cols] + rf[l, :, cols]) * factor
+            if k < n_out:
+                out_o[:, k * TILE:(k + 1) * TILE] = total[:, :TILE]
+            else:
+                conv_o[:, c0:c0 + TILE] = total
+            if size > TILE:
+                bias_o[...] = total[:8, TILE:]
+
+        @pl.when(place == 1)
+        def _():
+            both[0].wait_recv()
+            mine[:, :, cols] += rz[l, :, :, cols]
+            up.start()
+            down.wait_recv()
+            finish(1)
+
+        yield
+
+        @pl.when(place == 0)
+        def _():
+            up.wait_recv()
+            finish(0)
+            down.wait_send()
+
+        pl.when(place == 1)(up.wait_send)
+        pl.when(place == 2)(both[0].wait_send)
+        pl.when(place == 3)(both[1].wait_send)
+        yield
+
+    chunks = [[chunk(l, k) for k in range(tiles)] for l in range(2)]
+
+    def advance(l, *which):
+        if fused:
+            for k in which or range(tiles):
+                next(chunks[l][k])
+
+    def all_grads(l):
+        if fused:
+            return
+        for k in range(tiles):
+            grad_tile(l, k)
+        bias_grad(l)
+
     put_joined(0, B, 0, x[0, A, :])
-    put_joined(0, A, chan, x[0, A, :])
     put_joined(0, B, chan, x[0, B, :])
+    split_conv(0)
     forward(0, B)
+    split_out(0)
     second_b = second_input(B)
     pl.when(has_next)(x2_copy[1].start)
+    put_joined(0, A, chan, x[0, A, :])
     put_joined(1, B, chan, second_b)
-    split_weights(1)
+    late, early = pl.ds(chan, chan), pl.ds(0, chan)
+    fetches["sk"].wait()
     for r in (A, B):
         for l in range(2):
             put_outer(l, r, chan, sk[0, r, :])
-        put_outer(1, r, 0, c2[0, r, :])
-    late, early = pl.ds(chan, chan), pl.ds(0, chan)
-    for r in (A, B):
-        skip = split(sk[0, r, :])
-        dhs[0, r, :] = dot3(skip, (woh[0, :, late], wol[0, :, late]), NT)
-        dhs[1, r, :] = dot3(skip, (woh[1, :, late], wol[1, :, late]), NT) + dot3(
-            split(c2[0, r, :]), (woh[1, :, early], wol[1, :, early]), NT)
+        dhs[0, r, :] = dot3(split(sk[0, r, :]), (woh[0, :, late], wol[0, :, late]), NT)
     pl.when(has_prev)(t_copy.wait_recv)
     put_joined(0, A, 0, tail[...])
     forward(0, A)
     second_a = second_input(A)
     pl.when(has_next)(x2_copy[0].start)
     put_joined(1, A, chan, second_a)
+    split_conv(1)
+    split_out(1)
+    fetches["c2"].wait()
+    for r in (B, A):
+        put_outer(1, r, 0, c2[0, r, :])
+        dhs[1, r, :] = dot3(split(sk[0, r, :]), (woh[1, :, late], wol[1, :, late]), NT) + dot3(
+            split(c2[0, r, :]), (woh[1, :, early], wol[1, :, early]), NT)
     for i in (1, 0):
         r = (A, B)[i]
         pl.when(has_prev)(x2_copy[i].wait_recv)
@@ -236,45 +302,38 @@
         dmixed(1, r, dhs[1, r, :], i)
         q2[r, :] = back(1, r, 0)
         pl.when(has_prev)(q2_copy[i].start)
-    out_grads(1)
-    conv_grads(1)
-    if fused:
-        second_sums = sums(1)
-        next(second_sums)
-    out_later = []
+    all_grads(1)
+    advance(1)
     for i in (1, 0):
         r = (A, B)[i]
         c1[r, :] = c2[0, r, :] + back(1, r, chan)
-    if fused:
-        next(second_sums)
+    advance(1)
     for i in (1, 0):
         r = (A, B)[i]
         pl.when(has_next)(q2_copy[i].wait_recv)
         carried = c1[r, :] + q2r[r, :]
         c1[r, :] = carried
-        put_outer(0, r, 0, carried)
         dmixed(0, r, dhs[0, r, :] + dot3(split(carried), (woh[0, :, early], wol[0, :, early]), NT), i)
         q1[r, :] = back(0, r, 0)
         if i == 0:
             pl.when(has_prev)(q1_copy.start)
-    out_grads(0)
-    conv_grads(0)
-    if fused:
-        first_sums = sums(0)
-        next(first_sums)
-        next(second_sums)
+        put_outer(0, r, 0, carried)
+    all_grads(0)
+    for k in range(tiles):
+        advance(0, k)
+        advance(1, k)
+    advance(0)
+    advance(1)
     ig[0, A, :] = c1[A, :] + back(0, A, chan) + q1[B, :]
-    if fused:
-        next(first_sums)
     inner = c1[B, :] + back(0, B, chan)
     pl.when(has_next)(q1_copy.wait_recv)
     ig[0, B, :] = inner + q1r[...]
-    if fused:
-        next(second_sums)
-        next(first_sums)
-        next(first_sums)
-        next(second_sums)
-        next(first_sums)
+    for stage in range(3):
+        for k in range(tiles):
+            advance(0, k)
+            advance(1, k)
+    advance(0)
+    advance(0)
     pl.when(has_next)(t_copy.wait_send)
     for i in range(2):
         pl.when(has_next)(x2_copy[i].wait_send)
@@ -282,6 +341,15 @@
     pl.when(has_prev)(q1_copy.wait_send)
     for copy in copies:
         copy.wait_send()
+
+
+def hand_on(a, b, c, bias, a_out, b_out, c_out, bias_out, sems):
+    moves = [pltpu.make_async_copy(*pair, sems.at[i]) for i, pair in enumerate(((a, a_out), (b, b_out), (c, c_out)))]
+    for move in moves:
+        move.start()
+    bias_out[...] = bias[0, : bias_out.shape[0]]
+    for move in moves:
+        move.wait()
 
 
 def local(n_seq, n_dp, *args):
@@ -307,26 +375,36 @@
         vmem((rows, chan), F32), vmem((rows, chan), F32), vmem((half, chan), F32),
         vmem((rows, chan), F32), vmem((rows, chan), F32), vmem((rows, chan), F32),
         vmem((half, chan), F32), vmem((rows, chan), F32), vmem((2, 8, 2 * gate), F32),
-        pltpu.SemaphoreType.DMA((24,)), pltpu.SemaphoreType.DMA((24,)),
+        vmem(inputs.shape, F32), vmem(inputs.shape, F32),
+        vmem(convolution_weight.shape, F32), vmem(output_weight.shape, F32),
+        pltpu.SemaphoreType.DMA((6 + 36 * gate // TILE,)), pltpu.SemaphoreType.DMA((6 + 36 * gate // TILE,)),
+        pltpu.SemaphoreType.DMA((6,)),
     ]
     if fused:
         scratch += [
             vmem((2, 2, 2, 2, 2, block, width), F32), vmem((2, 2, 2, 2, block, width), F32),
-            vmem((2, 2, 2, block, width), F32), vmem((2, 2, 2, block, width), F32),
-            vmem((2, 4, block, width), F32),
+            vmem((2, 2, 2, block, width), F32), vmem((2, 2, block, width), F32),
+            vmem((2, 2, block, width), F32), vmem((2, block, width), F32),
         ]
-    spec = pl.BlockSpec(memory_space=pltpu.VMEM)
+    spec, anywhere = pl.BlockSpec(memory_space=pltpu.VMEM), pl.BlockSpec(memory_space=pl.ANY)
     input_grad, conv, out, bias = pl.pallas_call(
         functools.partial(kernel, n_seq, n_dp, fused, factor),
         out_shape=[sds(inputs.shape, F32)] + grads,
-        in_specs=[spec] * 6,
+        in_specs=[spec, anywhere, anywhere, anywhere, spec, anywhere],
         out_specs=[spec] * 4,
         scratch_shapes=scratch,
         compiler_params=pltpu.CompilerParams(
             collective_id=0, has_side_effects=True, vmem_limit_bytes=60 * 1024 * 1024),
     )(*args)
     if fused:
-        return input_grad, conv, out, bias[0, : 4 * gate // (n_seq * n_dp)]
+        piece = 4 * gate // (n_seq * n_dp)
+        return pl.pallas_call(
+            hand_on,
+            out_shape=[sds(inputs.shape, F32), *grads[:2], sds((piece,), F32)],
+            in_specs=[anywhere] * 3 + [spec],
+            out_specs=[anywhere] * 3 + [spec],
+            scratch_shapes=[pltpu.SemaphoreType.DMA((3,))],
+        )(input_grad, conv, out, bias)
 
     def scattered(terms):
         terms = terms.reshape((-1,) + terms.shape[2:]) * factor

time: 98.8 us -> 115 us (1.16); the launches traced: 97.8 us -> 115 us
  Pallas kernels: 91.1 us -> 114 us
  local copies, waits for them, and re-layouts: 6.1 us -> 0 us
    pallas_call x0 -> x1, Pallas kernels: none -> 24.2 us  [local(): pl.pallas_call(hand_on, out_shape=[sds(inputs.shape, F32), *grads[:2], sd...]
    unnamed x3 -> x0, local copies, waits for them, and re-layouts: 4.91 us -> none
    squeeze x1 -> x0, local copies, waits for them, and re-layouts: 1.2 us -> none  [local(): return (input_grad, conv, out, bias[0, :4 * gate // (n_seq * n_dp)])]
where the time goes in v2:
time: 115 us
  Pallas kernels  114 us (99%)
    pallas_call x1, Pallas kernels, local(): pl.pallas_call(functools.partial(kernel, n_seq, n_dp, fused, factor), out...  90.3 us
    pallas_call x1, Pallas kernels, local(): pl.pallas_call(hand_on, out_shape=[sds(inputs.shape, F32), *grads[:2], sd...  24.2 us

profile of v2, /device:TPU:0, one launch (start us, length us, event | category | flops | bytes accessed | tf_op | source)
XLA Modules:
  0.0 115.2 jit_solution(12126219754091978222)
XLA Ops:
  0.6 90.3 %shard_map.93 = (f32[1,512,256]{2,1,0:T(8,128)}, f32[32,1024]{1,0:T(8,128)}, f32[32,512]{1,0:T(8,128)}, f32[8,128]{1,0:T(8,128)}) custom-call(f32[1,512,256]{2,1,0:T(8,128)} %refs_0_.1, f32[1,512,256]{2,1,0:T(8,128)} %refs_1_.1, f32[1,512,256]{2,1,0:T(8,128)} %refs_2_.1, f32[2,512,1024]{2,1,0:T(8,128)} %refs_3_.1, f32[2,1024]{1,0:T(2,128)} %refs_4_.1, ...), custom_call_target="tpu_custom_call" | custom-call | tf_op jit(solution)/shard_map/pallas_call | solution.py:390
  90.9 24.2 %shard_map.94 = (f32[1,512,256]{2,1,0:T(8,128)}, f32[32,1024]{1,0:T(8,128)}, f32[32,512]{1,0:T(8,128)}, f32[64]{0:T(128)}) custom-call(f32[1,512,256]{2,1,0:T(8,128)} %get-tuple-element.8.a, f32[32,1024]{1,0:T(8,128)} %get-tuple-element.9.b, f32[32,512]{1,0:T(8,128)} %get-tuple-element.10.c, f32[8,128]{1,0:T(8,128)} %get-tuple-element.11.bias), custom_call_target="tpu_custom_call" | custom-call | tf_op jit(solution)/shard_map/pallas_call | solution.py:401

commit v3 on v2

--- a/solution.py
+++ b/solution.py
@@ -10,7 +10,6 @@
 
 F32, BF16 = jnp.float32, jnp.bfloat16
 NN = (((1,), (0,)), ((), ()))
-NT = (((1,), (1,)), ((), ()))
 TILE = 256
 
 
@@ -29,10 +28,10 @@
     refs = list(refs)
     x, c2_in, sk_in, cw_in, cb, ow_in = refs[:6]
     ig, conv_o, out_o, bias_o = refs[6:10]
-    (wch, wcl, woh, wol, jh, jl, jth, jtl, hh, hl, fa, ga, oth, otl, dhs, dzh, dzl,
-     x2, x2p, tail, q2, q2r, q1, q1r, c1, bsum, c2, sk, cw, ow, ssem, rsem, lsem) = refs[10:43]
+    (wch, wcl, woh, wol, wcth, wctl, woth, wotl, jh, jl, jth, jtl, hh, hl, fa, ga, oth, otl, dhs, dzh, dzl,
+     x2, x2p, tail, q2, q2r, q1, q1r, c1, bsum, c2, sk, cw, ow, ssem, rsem, lsem) = refs[10:47]
     if fused:
-        grad, rc, r1, r2, rz, rf = refs[43:]
+        grad, rc, r1, r2, rz, rf = refs[47:]
     rows, chan = x.shape[1], x.shape[2]
     half = rows // 2
     gate = ow_in.shape[1]
@@ -90,9 +89,18 @@
         fetches["ow%d" % l].wait()
         woh[l], wol[l] = split(ow[l])
 
-    def put_joined(l, r, c0, value):
+    def turn_conv(l):
+        wcth[l], wctl[l] = split(cw[l].T)
+
+    def turn_out(l):
+        woth[l], wotl[l] = split(ow[l].T)
+
+    def put_rows(l, r, c0, value):
         cols = pl.ds(c0, chan)
         jh[l, r, cols], jl[l, r, cols] = split(value)
+
+    def put_turned(l, r, c0, value):
+        cols = pl.ds(c0, chan)
         jth[l, cols, r], jtl[l, cols, r] = split(value.T)
 
     def put_outer(l, r, c0, value):
@@ -126,7 +134,7 @@
 
     def back(l, r, c0):
         taps = pl.ds(c0, chan)
-        return dot3((dzh[l, r, :], dzl[l, r, :]), (wch[l, taps, :], wcl[l, taps, :]), NT)
+        return dot3((dzh[l, r, :], dzl[l, r, :]), (wcth[l, :, taps], wctl[l, :, taps]), NN)
 
     def put_grad(l, kind, c0, value):
         if not fused:
@@ -266,68 +274,75 @@
             grad_tile(l, k)
         bias_grad(l)
 
-    put_joined(0, B, 0, x[0, A, :])
-    put_joined(0, B, chan, x[0, B, :])
+    every = pl.ds(0, rows)
+    put_rows(0, B, 0, x[0, A, :])
+    put_rows(0, B, chan, x[0, B, :])
     split_conv(0)
     forward(0, B)
     split_out(0)
     second_b = second_input(B)
     pl.when(has_next)(x2_copy[1].start)
-    put_joined(0, A, chan, x[0, A, :])
-    put_joined(1, B, chan, second_b)
+    put_rows(0, A, chan, x[0, A, :])
+    put_rows(1, B, chan, second_b)
     late, early = pl.ds(chan, chan), pl.ds(0, chan)
+    turn_out(0)
     fetches["sk"].wait()
-    for r in (A, B):
-        for l in range(2):
-            put_outer(l, r, chan, sk[0, r, :])
-        dhs[0, r, :] = dot3(split(sk[0, r, :]), (woh[0, :, late], wol[0, :, late]), NT)
+    skip = split(sk[0])
+    dhs[0] = dot3(skip, (woth[0, late, :], wotl[0, late, :]), NN)
     pl.when(has_prev)(t_copy.wait_recv)
-    put_joined(0, A, 0, tail[...])
+    put_rows(0, A, 0, tail[...])
     forward(0, A)
     second_a = second_input(A)
     pl.when(has_next)(x2_copy[0].start)
-    put_joined(1, A, chan, second_a)
+    put_rows(1, A, chan, second_a)
     split_conv(1)
     split_out(1)
+    turn_out(1)
     fetches["c2"].wait()
-    for r in (B, A):
-        put_outer(1, r, 0, c2[0, r, :])
-        dhs[1, r, :] = dot3(split(sk[0, r, :]), (woh[1, :, late], wol[1, :, late]), NT) + dot3(
-            split(c2[0, r, :]), (woh[1, :, early], wol[1, :, early]), NT)
+    dhs[1] = dot3(skip, (woth[1, late, :], wotl[1, late, :]), NN) + dot3(
+        split(c2[0]), (woth[1, early, :], wotl[1, early, :]), NN)
+    turn_conv(1)
     for i in (1, 0):
         r = (A, B)[i]
         pl.when(has_prev)(x2_copy[i].wait_recv)
-        put_joined(1, r, 0, x2p[r, :])
+        put_rows(1, r, 0, x2p[r, :])
         forward(1, r)
         dmixed(1, r, dhs[1, r, :], i)
         q2[r, :] = back(1, r, 0)
         pl.when(has_prev)(q2_copy[i].start)
+    for l in range(2):
+        put_outer(l, every, chan, sk[0])
+    put_outer(1, every, 0, c2[0])
+    put_turned(1, every, 0, x2p[...])
+    put_turned(1, every, chan, x2[...])
     all_grads(1)
     advance(1)
-    for i in (1, 0):
-        r = (A, B)[i]
-        c1[r, :] = c2[0, r, :] + back(1, r, chan)
+    c1[...] = c2[0] + back(1, every, chan)
+    turn_conv(0)
+    put_turned(0, B, 0, x[0, A, :])
+    put_turned(0, A, 0, tail[...])
+    put_turned(0, every, chan, x[0])
     advance(1)
     for i in (1, 0):
         r = (A, B)[i]
         pl.when(has_next)(q2_copy[i].wait_recv)
         carried = c1[r, :] + q2r[r, :]
         c1[r, :] = carried
-        dmixed(0, r, dhs[0, r, :] + dot3(split(carried), (woh[0, :, early], wol[0, :, early]), NT), i)
+        dmixed(0, r, dhs[0, r, :] + dot3(split(carried), (woth[0, early, :], wotl[0, early, :]), NN), i)
         q1[r, :] = back(0, r, 0)
         if i == 0:
             pl.when(has_prev)(q1_copy.start)
-        put_outer(0, r, 0, carried)
+    put_outer(0, every, 0, c1[...])
     all_grads(0)
     for k in range(tiles):
         advance(0, k)
         advance(1, k)
     advance(0)
     advance(1)
-    ig[0, A, :] = c1[A, :] + back(0, A, chan) + q1[B, :]
-    inner = c1[B, :] + back(0, B, chan)
+    c1[...] = c1[...] + back(0, every, chan)
+    ig[0, A, :] = c1[A, :] + q1[B, :]
     pl.when(has_next)(q1_copy.wait_recv)
-    ig[0, B, :] = inner + q1r[...]
+    ig[0, B, :] = c1[B, :] + q1r[...]
     for stage in range(3):
         for k in range(tiles):
             advance(0, k)
@@ -343,13 +358,9 @@
         copy.wait_send()
 
 
-def hand_on(a, b, c, bias, a_out, b_out, c_out, bias_out, sems):
-    moves = [pltpu.make_async_copy(*pair, sems.at[i]) for i, pair in enumerate(((a, a_out), (b, b_out), (c, c_out)))]
-    for move in moves:
-        move.start()
+def hand_on(a, b, c, bias, a_out, b_out, c_out, bias_out):
+    a_out[...], b_out[...], c_out[...] = a[...], b[...], c[...]
     bias_out[...] = bias[0, : bias_out.shape[0]]
-    for move in moves:
-        move.wait()
 
 
 def local(n_seq, n_dp, *args):
@@ -369,6 +380,7 @@
     pair = lambda *shape: [vmem(shape, BF16)] * 2
     scratch = [
         *pair(2, 2 * chan, 2 * gate), *pair(2, gate, 2 * chan),
+        *pair(2, 2 * gate, 2 * chan), *pair(2, 2 * chan, gate),
         *pair(2, rows, 2 * chan), *pair(2, 2 * chan, rows), *pair(2, rows, gate),
         vmem((2, rows, gate), F32), vmem((2, rows, gate), F32),
         *pair(2, 2 * chan, rows), vmem((2, rows, gate), F32), *pair(2, rows, 2 * gate),
@@ -401,9 +413,8 @@
         return pl.pallas_call(
             hand_on,
             out_shape=[sds(inputs.shape, F32), *grads[:2], sds((piece,), F32)],
-            in_specs=[anywhere] * 3 + [spec],
-            out_specs=[anywhere] * 3 + [spec],
-            scratch_shapes=[pltpu.SemaphoreType.DMA((3,))],
+            in_specs=[spec] * 4,
+            out_specs=[spec] * 4,
         )(input_grad, conv, out, bias)
 
     def scattered(terms):

time: 115 us -> 93.3 us (0.81)
  Pallas kernels: 114 us -> 92.5 us
    pallas_call x1, Pallas kernels: 24.2 us -> 1.98 us  [local(): pl.pallas_call(hand_on, out_shape=[sds(inputs.shape, F32), *grads[:2], sd...]
where the time goes in v3:
time: 93.3 us; the launch traced here: 93.2 us
  Pallas kernels  92.5 us (99%)
    pallas_call x1, Pallas kernels, local(): pl.pallas_call(functools.partial(kernel, n_seq, n_dp, fused, factor), out...  90.5 us
    pallas_call x1, Pallas kernels, local(): pl.pallas_call(hand_on, out_shape=[sds(inputs.shape, F32), *grads[:2], sd...  1.98 us

profile of v3, /device:TPU:0, one launch (start us, length us, event | category | flops | bytes accessed | tf_op | source)
XLA Modules:
  0.0 93.2 jit_solution(8183957573762938007)
XLA Ops:
  0.6 90.5 %shard_map.93 = (f32[1,512,256]{2,1,0:T(8,128)}, f32[32,1024]{1,0:T(8,128)}, f32[32,512]{1,0:T(8,128)}, f32[8,128]{1,0:T(8,128)}) custom-call(f32[1,512,256]{2,1,0:T(8,128)} %refs_0_.1, f32[1,512,256]{2,1,0:T(8,128)} %refs_1_.1, f32[1,512,256]{2,1,0:T(8,128)} %refs_2_.1, f32[2,512,1024]{2,1,0:T(8,128)} %refs_3_.1, f32[2,1024]{1,0:T(2,128)} %refs_4_.1, ...), custom_call_target="tpu_custom_call" | custom-call | tf_op jit(solution)/shard_map/pallas_call | solution.py:402
  91.2 2.0 %shard_map.94 = (f32[1,512,256]{2,1,0:T(8,128)}, f32[32,1024]{1,0:T(8,128)}, f32[32,512]{1,0:T(8,128)}, f32[64]{0:T(128)}) custom-call(f32[1,512,256]{2,1,0:T(8,128)} %get-tuple-element.8.a, f32[32,1024]{1,0:T(8,128)} %get-tuple-element.9.b, f32[32,512]{1,0:T(8,128)} %get-tuple-element.10.c, f32[8,128]{1,0:T(8,128)} %get-tuple-element.11.bias), custom_call_target="tpu_custom_call" | custom-call | tf_op jit(solution)/shard_map/pallas_call | solution.py:413

commit v4 on v3

--- a/solution.py
+++ b/solution.py
@@ -183,7 +183,7 @@
         if k == n_out - 1:
             size += 128
         cols = pl.ds(c0, size)
-        x_first = k % 2 == 0
+        x_first = l == 1 or k % 2 == 1
         other_c = (seq, 2 * me_x + 1 - me_c)
         other_x = (seq, 2 * (1 - me_x) + me_c)
         other_y = (2 * me_z + 1 - me_y, dp)
@@ -337,18 +337,18 @@
     for k in range(tiles):
         advance(0, k)
         advance(1, k)
-    advance(0)
-    advance(1)
+        if k > 1:
+            advance(0, k - 2)
+    advance(0, tiles - 2, tiles - 1)
     c1[...] = c1[...] + back(0, every, chan)
     ig[0, A, :] = c1[A, :] + q1[B, :]
     pl.when(has_next)(q1_copy.wait_recv)
     ig[0, B, :] = c1[B, :] + q1r[...]
-    for stage in range(3):
-        for k in range(tiles):
-            advance(0, k)
-            advance(1, k)
-    advance(0)
-    advance(0)
+    for tick in range(tiles + 6):
+        for l, starts in ((1, (0, 1, 2, 3)), (0, (0, 2, 3, 4, 5))):
+            for start in reversed(starts):
+                if 0 <= tick - start < tiles:
+                    advance(l, tick - start)
     pl.when(has_next)(t_copy.wait_send)
     for i in range(2):
         pl.when(has_next)(x2_copy[i].wait_send)

time: 93.3 us -> 104 us (1.11); the launches traced: 93.2 us -> 103 us
  Pallas kernels: 92.5 us -> 102 us
    pallas_call x1, Pallas kernels: 90.5 us -> 100 us  [local(): pl.pallas_call(functools.partial(kernel, n_seq, n_dp, fused, factor), out...]
where the time goes in v4:
time: 104 us; the launch traced here: 103 us
  Pallas kernels  102 us (98%)
    pallas_call x1, Pallas kernels, local(): pl.pallas_call(functools.partial(kernel, n_seq, n_dp, fused, factor), out...  100 us

profile of v4, /device:TPU:0, one launch (start us, length us, event | category | flops | bytes accessed | tf_op | source)
XLA Modules:
  0.0 102.7 jit_solution(11111550248439345514)
XLA Ops:
  0.6 100.0 %shard_map.93 = (f32[1,512,256]{2,1,0:T(8,128)}, f32[32,1024]{1,0:T(8,128)}, f32[32,512]{1,0:T(8,128)}, f32[8,128]{1,0:T(8,128)}) custom-call(f32[1,512,256]{2,1,0:T(8,128)} %refs_0_.1, f32[1,512,256]{2,1,0:T(8,128)} %refs_1_.1, f32[1,512,256]{2,1,0:T(8,128)} %refs_2_.1, f32[2,512,1024]{2,1,0:T(8,128)} %refs_3_.1, f32[2,1024]{1,0:T(2,128)} %refs_4_.1, ...), custom_call_target="tpu_custom_call" | custom-call | tf_op jit(solution)/shard_map/pallas_call | solution.py:402
  100.7 2.0 %shard_map.94 = (f32[1,512,256]{2,1,0:T(8,128)}, f32[32,1024]{1,0:T(8,128)}, f32[32,512]{1,0:T(8,128)}, f32[64]{0:T(128)}) custom-call(f32[1,512,256]{2,1,0:T(8,128)} %get-tuple-element.8.a, f32[32,1024]{1,0:T(8,128)} %get-tuple-element.9.b, f32[32,512]{1,0:T(8,128)} %get-tuple-element.10.c, f32[8,128]{1,0:T(8,128)} %get-tuple-element.11.bias), custom_call_target="tpu_custom_call" | custom-call | tf_op jit(solution)/shard_map/pallas_call | solution.py:413

commit v5 on v4

v5 whole, which is shorter than its diff:
```python
import functools
import math

import jax
import jax.numpy as jnp
from jax import lax
from jax.experimental import pallas as pl
from jax.experimental.pallas import tpu as pltpu
from jax.sharding import PartitionSpec as P

F32, BF16 = jnp.float32, jnp.bfloat16
NN = (((1,), (0,)), ((), ()))
TILE = 256


def split(value):
    high = value.astype(BF16)
    return high, (value - high.astype(F32)).astype(BF16)


def dot3(left, right, dims):
    product = functools.partial(lax.dot_general, dimension_numbers=dims, preferred_element_type=F32)
    (lh, ll), (rh, rl) = left, right
    return (product(ll, rh) + product(lh, rl)) + product(lh, rh)


def kernel(n_seq, n_dp, fused, factor, *refs):
    refs = list(refs)
    x, c2_in, sk_in, cw_in, cb, ow_in = refs[:6]
    ig, conv_o, out_o, bias_o = refs[6:10]
    (wch, wcl, woh, wol, wcth, wctl, woth, wotl, jh, jl, jth, jtl, hh, hl, fa, ga, oth, otl, dhs, dzh, dzl,
     x2, x2p, tail, q2, q2r, q1, q1r, c1, bsum, c2, sk, cw, ow, ssem, rsem, lsem) = refs[10:47]
    if fused:
        grad, rc, r1, r2, rz, rf = refs[47:53]
        bias_refs, sums = refs[53:59], refs[59]
    rows, chan = x.shape[1], x.shape[2]
    half = rows // 2
    gate = ow_in.shape[1]
    A, B = pl.ds(0, half), pl.ds(half, half)

    seq, dp = lax.axis_index("seq"), lax.axis_index("dp")
    has_next, has_prev = seq < n_seq - 1, seq > 0
    nxt, prv = lax.rem(seq + 1, n_seq), lax.rem(seq + n_seq - 1, n_seq)
    me_z, me_y, me_x, me_c = seq // 2, seq % 2, dp // 2, dp % 2

    fetches = {}
    for i, (name, src, dst) in enumerate((
        ("cw0", cw_in.at[0], cw.at[0]), ("ow0", ow_in.at[0], ow.at[0]), ("sk", sk_in, sk),
        ("c2", c2_in, c2), ("ow1", ow_in.at[1], ow.at[1]), ("cw1", cw_in.at[1], cw.at[1]))):
        fetches[name] = pltpu.make_async_copy(src, dst, lsem.at[i])
        fetches[name].start()

    barrier = pltpu.get_barrier_semaphore()
    greet = [(nxt, dp), (prv, dp)]
    if fused:
        greet += [(seq, 2 * me_x + 1 - me_c), (seq, 2 * (1 - me_x) + me_c), (2 * me_z + 1 - me_y, dp)]
        greet += [(lax.rem(seq + 2 * k, n_seq), dp) for k in range(1, n_seq // 2)]
    for s, d in greet:
        pl.semaphore_signal(barrier, inc=1, device_id=(s, d), device_id_type=pl.DeviceIdType.MESH)
    pl.semaphore_wait(barrier, len(greet))

    def remote(src, dst, send, recv, s, d):
        return pltpu.make_async_remote_copy(
            src_ref=src, dst_ref=dst, send_sem=ssem.at[send], recv_sem=rsem.at[recv],
            device_id=(s, d), device_id_type=pl.DeviceIdType.MESH)

    t_copy = remote(x.at[0, B], tail, 0, 0, nxt, dp)
    x2_copy = [remote(x2.at[r], x2p.at[r], 1 + i, 1 + i, nxt, dp) for i, r in enumerate((A, B))]
    q2_copy = [remote(q2.at[r], q2r.at[r], 3 + i, 3 + i, prv, dp) for i, r in enumerate((A, B))]
    q1_copy = remote(q1.at[A], q1r, 5, 5, prv, dp)

    pl.when(has_next)(t_copy.start)

    @pl.when(jnp.logical_not(has_prev))
    def _():
        tail[...] = jnp.zeros_like(tail)
        x2p[...] = jnp.zeros_like(x2p)

    @pl.when(jnp.logical_not(has_next))
    def _():
        q2r[...] = jnp.zeros_like(q2r)
        q1r[...] = jnp.zeros_like(q1r)

    def tiled(extent, body, size=TILE):
        @pl.loop(0, extent // size)
        def _(n):
            body(pl.ds(pl.multiple_of(n * size, size), size))

    def split_conv(l):
        fetches["cw%d" % l].wait()

        def body(r):
            wch[l, r, :], wcl[l, r, :] = split(cw[l, r, :])
        tiled(2 * chan, body, 64)

    def split_out(l):
        fetches["ow%d" % l].wait()

        def body(r):
            woh[l, r, :], wol[l, r, :] = split(ow[l, r, :])
        tiled(gate, body, 64)

    def turn_conv(l):
        def body(r):
            wcth[l, r, :], wctl[l, r, :] = split(cw[l, :, r].T)
        tiled(2 * gate, body)

    def turn_out(l):
        def body(r):
            woth[l, r, :], wotl[l, r, :] = split(ow[l, :, r].T)
        tiled(2 * chan, body)

    def put_rows(l, r, c0, value):
        cols = pl.ds(c0, chan)
        jh[l, r, cols], jl[l, r, cols] = split(value)

    def put_turned(l, r, c0, value):
        cols = pl.ds(c0, chan)
        jth[l, cols, r], jtl[l, cols, r] = split(value.T)

    def put_outer(l, r, c0, value):
        cols = pl.ds(c0, chan)
        oth[l, cols, r], otl[l, cols, r] = split(value.T)

    def forward(l, r):
        @pl.loop(0, gate // TILE)
        def _(n):
            joined = (jh[l, r, :], jl[l, r, :])
            cols = pl.ds(pl.multiple_of(n * TILE, TILE), TILE)
            gcols = pl.ds(pl.multiple_of(gate + n * TILE, TILE), TILE)
            f = dot3(joined, (wch[l, :, cols], wcl[l, :, cols]), NN) + cb[l:l + 1, cols]
            g = dot3(joined, (wch[l, :, gcols], wcl[l, :, gcols]), NN) + cb[l:l + 1, gcols]
            t, s = jnp.tanh(f), jax.nn.sigmoid(g)
            h = t * s
            fa[l, r, cols] = s * (1.0 - t * t)
            ga[l, r, cols] = h * (1.0 - s)
            hh[l, r, cols], hl[l, r, cols] = split(h)

    def second_input(r):
        out = pl.ds(0, chan)
        value = x[0, r, :] + dot3((hh[0, r, :], hl[0, r, :]), (woh[0, :, out], wol[0, :, out]), NN)
        x2[r, :] = value
        return value

    def dmixed(l, r):
        @pl.loop(0, gate // TILE)
        def _(n):
            cols = pl.ds(pl.multiple_of(n * TILE, TILE), TILE)
            gcols = pl.ds(pl.multiple_of(gate + n * TILE, TILE), TILE)
            dh = dhs[l, r, cols]
            for part, where in ((dh * fa[l, r, cols], cols), (dh * ga[l, r, cols], gcols)):
                dzh[l, r, where], dzl[l, r, where] = split(part)
                total = jnp.sum(part, axis=0, keepdims=True)
                bsum[l, 0:1, where] = bsum[l, 0:1, where] + total

    def back(l, r, c0):
        taps = pl.ds(c0, chan)
        return dot3((dzh[l, r, :], dzl[l, r, :]), (wcth[l, :, taps], wctl[l, :, taps]), NN)

    n_out, n_conv = gate // TILE, 2 * gate // TILE
    tiles = n_out + n_conv

    def put_grad(l, kind, n, value):
        if not fused:
            (conv_o if kind == 0 else out_o)[l, :, pl.ds(pl.multiple_of(n * TILE, TILE), TILE)] = value
            return
        block = value.shape[0] // 16
        for j in range(16):
            grad[l, kind * n_conv + n, j % 2, j // 2 % 2, j // 4 % 2, j // 8] = value[j * block:(j + 1) * block]

    def gradients(l):
        @pl.loop(0, n_out)
        def _(n):
            cols = pl.ds(pl.multiple_of(n * TILE, TILE), TILE)
            put_grad(l, 1, n, dot3((oth[l], otl[l]), (hh[l, :, cols], hl[l, :, cols]), NN))
            step(l, n_conv + n, 0, "core")

        @pl.loop(0, n_conv)
        def _(n):
            cols = pl.ds(pl.multiple_of(n * TILE, TILE), TILE)
            put_grad(l, 0, n, dot3((jth[l], jtl[l]), (dzh[l, :, cols], dzl[l, :, cols]), NN))
            step(l, n, 0, "core")

        total = bsum[l, 0:1, :]
        if not fused:
            bias_o[l:l + 1, :] = total
            return
        piece, terms = 2 * gate // 16, bias_refs[0]
        terms[l] = jnp.zeros(terms.shape[1:], F32)
        for j in range(16):
            terms[l, j % 2, j // 2 % 2, j // 4 % 2, j // 8, 0:1, 0:piece] = total[:, j * piece:(j + 1) * piece]
        step(l, None, 0, "core")

    def step(l, k, odd, what):
        if not fused:
            return
        if k is None:
            mine, got_c, got_1, got_2, got_z, got_f = (ref.at[l] for ref in bias_refs)
            base = 6 + 6 * (2 * tiles + l)
        else:
            mine, got_c, got_1, got_2, got_z, got_f = (ref.at[l, k] for ref in (grad, rc, r1, r2, rz, rf))
            base = 6 + 6 * (tiles * l + k)
        other_c = (seq, 2 * me_x + 1 - me_c)
        other_x = (seq, 2 * (1 - me_x) + me_c)
        other_y = (2 * me_z + 1 - me_y, dp)
        place = me_z if l == 0 else 3 - me_z
        low = lambda p: p if l == 0 else 1 - p
        at_place = lambda p: (2 * (p if l == 0 else 3 - p) + me_y, dp)
        own = mine.at[me_c]
        last = own.at[me_x, me_y]
        core = remote(mine.at[1 - me_c], got_c, base, base, *other_c)
        if odd:
            first = remote(own.at[:, 1 - me_y], got_1, base + 1, base + 1, *other_y)
            second = remote(own.at[1 - me_x, me_y], got_2, base + 2, base + 2, *other_x)
        else:
            first = remote(own.at[1 - me_x], got_1, base + 1, base + 1, *other_x)
            second = remote(own.at[me_x, 1 - me_y], got_2, base + 2, base + 2, *other_y)
        to_1, to_2 = (remote(last, got_z, base + 3, base + 3, *at_place(p)) for p in (1, 2))
        up = remote(last.at[low(0)], got_f, base + 3, base + 4, *at_place(0))
        down = remote(last.at[low(1)], got_f, base + 3, base + 4, *at_place(1))

        def finish(p):
            total = (last[low(p)] + got_f[...]) * factor
            if k is None:
                bias_o[...] = total
            else:
                sums[k] = total

        if what == "core":
            core.start()
        elif what == "first":
            core.wait_recv()
            own[...] += got_c[...]
            first.start()
        elif what == "second":
            first.wait_recv()
            if odd:
                own[:, me_y] += got_1[...]
            else:
                own[me_x] += got_1[...]
            second.start()
        elif what == "z":
            second.wait_recv()
            last[...] += got_2[...]
            pl.when(place == 3)(to_2.start)
            pl.when(place == 0)(down.start)
        elif what == "relay":
            @pl.when(place == 2)
            def _():
                to_2.wait_recv()
                last[...] += got_z[...]
                to_1.start()
        elif what == "owner":
            @pl.when(place == 1)
            def _():
                to_1.wait_recv()
                last[...] += got_z[...]
                up.start()
                down.wait_recv()
                finish(1)
        elif what == "end":
            @pl.when(place == 0)
            def _():
                up.wait_recv()
                finish(0)
                down.wait_send()

            pl.when(place == 1)(up.wait_send)
            pl.when(place == 2)(to_1.wait_send)
            pl.when(place == 3)(to_2.wait_send)
            core.wait_send()
            first.wait_send()
            second.wait_send()

    def advance(*moves):
        if not fused:
            return
        longest = max(behind for _, _, behind in moves)

        @pl.loop(0, tiles // 2 + longest)
        def _(tick):
            for l, what, behind in moves:
                def body(l=l, what=what, behind=behind):
                    for odd in range(2):
                        step(l, 2 * (tick - behind) + odd, odd, what)
                if longest == 0:
                    body()
                else:
                    pl.when(jnp.logical_and(tick >= behind, tick < behind + tiles // 2))(body)

        for l, what, _ in moves:
            step(l, None, 0, what)

    bsum[...] = jnp.zeros_like(bsum)
    every = pl.ds(0, rows)
    put_rows(0, B, 0, x[0, A, :])
    put_rows(0, B, chan, x[0, B, :])
    split_conv(0)
    forward(0, B)
    split_out(0)
    second_b = second_input(B)
    pl.when(has_next)(x2_copy[1].start)
    put_rows(0, A, chan, x[0, A, :])
    put_rows(1, B, chan, second_b)
    late, early = pl.ds(chan, chan), pl.ds(0, chan)
    turn_out(0)
    fetches["sk"].wait()
    skip = split(sk[0])
    dhs[0] = dot3(skip, (woth[0, late, :], wotl[0, late, :]), NN)
    pl.when(has_prev)(t_copy.wait_recv)
    put_rows(0, A, 0, tail[...])
    forward(0, A)
    second_a = second_input(A)
    pl.when(has_next)(x2_copy[0].start)
    put_rows(1, A, chan, second_a)
    split_conv(1)
    split_out(1)
    turn_out(1)
    fetches["c2"].wait()
    dhs[1] = dot3(skip, (woth[1, late, :], wotl[1, late, :]), NN) + dot3(
        split(c2[0]), (woth[1, early, :], wotl[1, early, :]), NN)
    turn_conv(1)
    def half_copy(src, dst, base, i, peer):
        r = pl.ds(pl.multiple_of(i * half, half), half)
        return r, remote(src.at[r], dst.at[r], base + i, base + i, peer, dp)

    @pl.loop(0, 2)
    def _(n):
        r, landed = half_copy(x2, x2p, 1, 1 - n, nxt)
        pl.when(has_prev)(landed.wait_recv)
        put_rows(1, r, 0, x2p[r, :])
        forward(1, r)
        dmixed(1, r)
        q2[r, :] = back(1, r, 0)
        _, leaving = half_copy(q2, q2r, 3, 1 - n, prv)
        pl.when(has_prev)(leaving.start)

    @pl.loop(0, 2)
    def _(n):
        r = pl.ds(pl.multiple_of(n * half, half), half)
        for l in range(2):
            put_outer(l, r, chan, sk[0, r, :])
        put_outer(1, r, 0, c2[0, r, :])
        put_turned(1, r, 0, x2p[r, :])
        put_turned(1, r, chan, x2[r, :])

    gradients(1)

    @pl.loop(0, 2)
    def _(n):
        r = pl.ds(pl.multiple_of(n * half, half), half)
        c1[r, :] = c2[0, r, :] + back(1, r, chan)
        put_turned(0, r, chan, x[0, r, :])

    turn_conv(0)
    put_turned(0, B, 0, x[0, A, :])
    put_turned(0, A, 0, tail[...])
    advance((1, "first", 0))

    @pl.loop(0, 2)
    def _(n):
        r, landed = half_copy(q2, q2r, 3, 1 - n, prv)
        pl.when(has_next)(landed.wait_recv)
        carried = c1[r, :] + q2r[r, :]
        c1[r, :] = carried
        dhs[0, r, :] += dot3(split(carried), (woth[0, early, :], wotl[0, early, :]), NN)
        dmixed(0, r)
        q1[r, :] = back(0, r, 0)

    pl.when(has_prev)(q1_copy.start)

    @pl.loop(0, 2)
    def _(n):
        r = pl.ds(pl.multiple_of(n * half, half), half)
        put_outer(0, r, 0, c1[r, :])

    gradients(0)
    advance((0, "first", 0))
    advance((1, "second", 0))

    @pl.loop(0, 2)
    def _(n):
        r = pl.ds(pl.multiple_of(n * half, half), half)
        c1[r, :] += back(0, r, chan)

    ig[0, A, :] = c1[A, :] + q1[B, :]
    pl.when(has_next)(q1_copy.wait_recv)
    ig[0, B, :] = c1[B, :] + q1r[...]
    advance((1, "z", 0), (0, "second", 0), (1, "relay", 1), (0, "z", 1), (1, "owner", 2), (0, "relay", 2))
    advance((0, "owner", 0))
    advance((0, "end", 0))
    advance((1, "end", 0))
    if fused:
        for n in range(n_conv):
            conv_o[:, n * TILE:(n + 1) * TILE] = sums[n]
        for n in range(n_out):
            out_o[:, n * TILE:(n + 1) * TILE] = sums[n_conv + n]
    pl.when(has_next)(t_copy.wait_send)
    for i in range(2):
        pl.when(has_next)(x2_copy[i].wait_send)
        pl.when(has_prev)(q2_copy[i].wait_send)
    pl.when(has_prev)(q1_copy.wait_send)


def hand_on(a, b, c, bias, a_out, b_out, c_out, bias_out):
    a_out[...], b_out[...], c_out[...] = a[...], b[...], c[...]
    bias_out[...] = bias[0, : bias_out.shape[0]]


def local(n_seq, n_dp, *args):
    inputs, _, _, convolution_weight, _, output_weight = args
    _, rows, chan = inputs.shape
    half = rows // 2
    gate = output_weight.shape[1]
    fused = (n_seq, n_dp) == (8, 4)
    factor = 1.0 / math.sqrt(rows * n_seq * n_dp)
    block = 2 * (2 * chan) // (n_seq * n_dp)
    vmem, sds = pltpu.VMEM, jax.ShapeDtypeStruct
    if fused:
        grads = [sds((block, 2 * gate), F32), sds((block, gate), F32), sds((8, 128), F32)]
    else:
        grads = [sds((2, 2 * chan, 2 * gate), F32), sds((2, 2 * chan, gate), F32), sds((2, 2 * gate), F32)]
    pair = lambda *shape: [vmem(shape, BF16)] * 2
    scratch = [
        *pair(2, 2 * chan, 2 * gate), *pair(2, gate, 2 * chan),
        *pair(2, 2 * gate, 2 * chan), *pair(2, 2 * chan, gate),
        *pair(2, rows, 2 * chan), *pair(2, 2 * chan, rows), *pair(2, rows, gate),
        vmem((2, rows, gate), F32), vmem((2, rows, gate), F32),
        *pair(2, 2 * chan, rows), vmem((2, rows, gate), F32), *pair(2, rows, 2 * gate),
        vmem((rows, chan), F32), vmem((rows, chan), F32), vmem((half, chan), F32),
        vmem((rows, chan), F32), vmem((rows, chan), F32), vmem((rows, chan), F32),
        vmem((half, chan), F32), vmem((rows, chan), F32), vmem((2, 8, 2 * gate), F32),
        vmem(inputs.shape, F32), vmem(inputs.shape, F32),
        vmem(convolution_weight.shape, F32), vmem(output_weight.shape, F32),
        pltpu.SemaphoreType.DMA((18 + 36 * gate // TILE,)), pltpu.SemaphoreType.DMA((18 + 36 * gate // TILE,)),
        pltpu.SemaphoreType.DMA((6,)),
    ]
    if fused:
        tiles = 3 * gate // 256
        for lead, tile in (((2, tiles), (block, 256)), ((2,), (8, 128))):
            for between in ((2, 2, 2, 2), (2, 2, 2), (2, 2), (2,), (2,), ()):
                scratch.append(vmem(lead + between + tile, F32))
        scratch.append(vmem((tiles, block, 256), F32))
    spec, anywhere = pl.BlockSpec(memory_space=pltpu.VMEM), pl.BlockSpec(memory_space=pl.ANY)
    input_grad, conv, out, bias = pl.pallas_call(
        functools.partial(kernel, n_seq, n_dp, fused, factor),
        out_shape=[sds(inputs.shape, F32)] + grads,
        in_specs=[spec, anywhere, anywhere, anywhere, spec, anywhere],
        out_specs=[spec] * 4,
        scratch_shapes=scratch,
        compiler_params=pltpu.CompilerParams(
            collective_id=0, has_side_effects=True, vmem_limit_bytes=60 * 1024 * 1024),
    )(*args)
    if fused:
        piece = 4 * gate // (n_seq * n_dp)
        return pl.pallas_call(
            hand_on,
            out_shape=[sds(inputs.shape, F32), *grads[:2], sds((piece,), F32)],
            in_specs=[spec] * 4,
            out_specs=[spec] * 4,
        )(input_grad, conv, out, bias)

    def scattered(terms):
        terms = terms.reshape((-1,) + terms.shape[2:]) * factor
        part = lax.psum_scatter(terms, "seq", scatter_dimension=0, tiled=True)
        return lax.psum_scatter(part, "dp", scatter_dimension=0, tiled=True)

    return input_grad, scattered(conv), scattered(out), scattered(bias)


def solution(mesh):
    return jax.shard_map(
        functools.partial(local, mesh.shape["seq"], mesh.shape["dp"]),
        mesh=mesh,
        in_specs=(P("dp", "seq", None),) * 3 + (P(), P(), P()),
        out_specs=(P("dp", "seq", None), P(("seq", "dp"), None), P(("seq", "dp"), None), P(("seq", "dp"))),
        check_vma=False,
    )
```

time: 104 us -> 98.4 us (0.946); the launches traced: 103 us -> 98.3 us
  Pallas kernels: 102 us -> 97.6 us
    pallas_call x1, Pallas kernels: 100 us -> 95.6 us  [local(): pl.pallas_call(functools.partial(kernel, n_seq, n_dp, fused, factor), out...]
where the time goes in v5:
time: 98.4 us; the launch traced here: 98.3 us
  Pallas kernels  97.6 us (99%)
    pallas_call x1, Pallas kernels, local(): pl.pallas_call(functools.partial(kernel, n_seq, n_dp, fused, factor), out...  95.6 us
    pallas_call x1, Pallas kernels, local(): pl.pallas_call(hand_on, out_shape=[sds(inputs.shape, F32), *grads[:2], sd...  1.98 us

profile of v5, /device:TPU:0, one launch (start us, length us, event | category | flops | bytes accessed | tf_op | source)
XLA Modules:
  0.0 98.3 jit_solution(13847146162780082277)
XLA Ops:
  0.6 95.6 %shard_map.93 = (f32[1,512,256]{2,1,0:T(8,128)}, f32[32,1024]{1,0:T(8,128)}, f32[32,512]{1,0:T(8,128)}, f32[8,128]{1,0:T(8,128)}) custom-call(f32[1,512,256]{2,1,0:T(8,128)} %refs_0_.1, f32[1,512,256]{2,1,0:T(8,128)} %refs_1_.1, f32[1,512,256]{2,1,0:T(8,128)} %refs_2_.1, f32[2,512,1024]{2,1,0:T(8,128)} %refs_3_.1, f32[2,1024]{1,0:T(2,128)} %refs_4_.1, ...), custom_call_target="tpu_custom_call" | custom-call | tf_op jit(solution)/shard_map/pallas_call | solution.py:445
  96.3 2.0 %shard_map.94 = (f32[1,512,256]{2,1,0:T(8,128)}, f32[32,1024]{1,0:T(8,128)}, f32[32,512]{1,0:T(8,128)}, f32[64]{0:T(128)}) custom-call(f32[1,512,256]{2,1,0:T(8,128)} %get-tuple-element.8.a, f32[32,1024]{1,0:T(8,128)} %get-tuple-element.9.b, f32[32,512]{1,0:T(8,128)} %get-tuple-element.10.c, f32[8,128]{1,0:T(8,128)} %get-tuple-element.11.bias), custom_call_target="tpu_custom_call" | custom-call | tf_op jit(solution)/shard_map/pallas_call | solution.py:456

commit v6 on v5

--- a/solution.py
+++ b/solution.py
@@ -13,6 +13,10 @@
 TILE = 256
 
 
+def unrolled(start, stop):
+    return lambda body: [body(n) for n in range(start, stop)]
+
+
 def split(value):
     high = value.astype(BF16)
     return high, (value - high.astype(F32)).astype(BF16)
@@ -82,23 +86,23 @@
         q1r[...] = jnp.zeros_like(q1r)
 
     def tiled(extent, body, size=TILE):
-        @pl.loop(0, extent // size)
+        @unrolled(0, extent // size)
         def _(n):
-            body(pl.ds(pl.multiple_of(n * size, size), size))
+            body(pl.ds(n * size, size))
 
     def split_conv(l):
         fetches["cw%d" % l].wait()
 
         def body(r):
             wch[l, r, :], wcl[l, r, :] = split(cw[l, r, :])
-        tiled(2 * chan, body, 64)
+        tiled(2 * chan, body)
 
     def split_out(l):
         fetches["ow%d" % l].wait()
 
         def body(r):
             woh[l, r, :], wol[l, r, :] = split(ow[l, r, :])
-        tiled(gate, body, 64)
+        tiled(gate, body)
 
     def turn_conv(l):
         def body(r):
@@ -123,11 +127,11 @@
         oth[l, cols, r], otl[l, cols, r] = split(value.T)
 
     def forward(l, r):
-        @pl.loop(0, gate // TILE)
+        @unrolled(0, gate // TILE)
         def _(n):
             joined = (jh[l, r, :], jl[l, r, :])
-            cols = pl.ds(pl.multiple_of(n * TILE, TILE), TILE)
-            gcols = pl.ds(pl.multiple_of(gate + n * TILE, TILE), TILE)
+            cols = pl.ds(n * TILE, TILE)
+            gcols = pl.ds(gate + n * TILE, TILE)
             f = dot3(joined, (wch[l, :, cols], wcl[l, :, cols]), NN) + cb[l:l + 1, cols]
             g = dot3(joined, (wch[l, :, gcols], wcl[l, :, gcols]), NN) + cb[l:l + 1, gcols]
             t, s = jnp.tanh(f), jax.nn.sigmoid(g)
@@ -143,10 +147,10 @@
         return value
 
     def dmixed(l, r):
-        @pl.loop(0, gate // TILE)
+        @unrolled(0, gate // TILE)
         def _(n):
-            cols = pl.ds(pl.multiple_of(n * TILE, TILE), TILE)
-            gcols = pl.ds(pl.multiple_of(gate + n * TILE, TILE), TILE)
+            cols = pl.ds(n * TILE, TILE)
+            gcols = pl.ds(gate + n * TILE, TILE)
             dh = dhs[l, r, cols]
             for part, where in ((dh * fa[l, r, cols], cols), (dh * ga[l, r, cols], gcols)):
                 dzh[l, r, where], dzl[l, r, where] = split(part)
@@ -162,22 +166,22 @@
 
     def put_grad(l, kind, n, value):
         if not fused:
-            (conv_o if kind == 0 else out_o)[l, :, pl.ds(pl.multiple_of(n * TILE, TILE), TILE)] = value
+            (conv_o if kind == 0 else out_o)[l, :, pl.ds(n * TILE, TILE)] = value
             return
         block = value.shape[0] // 16
         for j in range(16):
             grad[l, kind * n_conv + n, j % 2, j // 2 % 2, j // 4 % 2, j // 8] = value[j * block:(j + 1) * block]
 
     def gradients(l):
-        @pl.loop(0, n_out)
+        @unrolled(0, n_out)
         def _(n):
-            cols = pl.ds(pl.multiple_of(n * TILE, TILE), TILE)
+            cols = pl.ds(n * TILE, TILE)
             put_grad(l, 1, n, dot3((oth[l], otl[l]), (hh[l, :, cols], hl[l, :, cols]), NN))
             step(l, n_conv + n, 0, "core")
 
-        @pl.loop(0, n_conv)
+        @unrolled(0, n_conv)
         def _(n):
-            cols = pl.ds(pl.multiple_of(n * TILE, TILE), TILE)
+            cols = pl.ds(n * TILE, TILE)
             put_grad(l, 0, n, dot3((jth[l], jtl[l]), (dzh[l, :, cols], dzl[l, :, cols]), NN))
             step(l, n, 0, "core")
 
@@ -272,24 +276,9 @@
             first.wait_send()
             second.wait_send()
 
-    def advance(*moves):
-        if not fused:
-            return
-        longest = max(behind for _, _, behind in moves)
-
-        @pl.loop(0, tiles // 2 + longest)
-        def _(tick):
-            for l, what, behind in moves:
-                def body(l=l, what=what, behind=behind):
-                    for odd in range(2):
-                        step(l, 2 * (tick - behind) + odd, odd, what)
-                if longest == 0:
-                    body()
-                else:
-                    pl.when(jnp.logical_and(tick >= behind, tick < behind + tiles // 2))(body)
-
-        for l, what, _ in moves:
-            step(l, None, 0, what)
+    def advance(l, what, which=range(tiles + 1)):
+        for k in which:
+            step(l, k if k < tiles else None, k % 2, what)
 
     bsum[...] = jnp.zeros_like(bsum)
     every = pl.ds(0, rows)
@@ -321,10 +310,10 @@
         split(c2[0]), (woth[1, early, :], wotl[1, early, :]), NN)
     turn_conv(1)
     def half_copy(src, dst, base, i, peer):
-        r = pl.ds(pl.multiple_of(i * half, half), half)
+        r = pl.ds(i * half, half)
         return r, remote(src.at[r], dst.at[r], base + i, base + i, peer, dp)
 
-    @pl.loop(0, 2)
+    @unrolled(0, 2)
     def _(n):
         r, landed = half_copy(x2, x2p, 1, 1 - n, nxt)
         pl.when(has_prev)(landed.wait_recv)
@@ -335,9 +324,9 @@
         _, leaving = half_copy(q2, q2r, 3, 1 - n, prv)
         pl.when(has_prev)(leaving.start)
 
-    @pl.loop(0, 2)
-    def _(n):
-        r = pl.ds(pl.multiple_of(n * half, half), half)
+    @unrolled(0, 2)
+    def _(n):
+        r = pl.ds(n * half, half)
         for l in range(2):
             put_outer(l, r, chan, sk[0, r, :])
         put_outer(1, r, 0, c2[0, r, :])
@@ -346,18 +335,19 @@
 
     gradients(1)
 
-    @pl.loop(0, 2)
-    def _(n):
-        r = pl.ds(pl.multiple_of(n * half, half), half)
+    @unrolled(0, 2)
+    def _(n):
+        r = pl.ds(n * half, half)
         c1[r, :] = c2[0, r, :] + back(1, r, chan)
         put_turned(0, r, chan, x[0, r, :])
 
     turn_conv(0)
     put_turned(0, B, 0, x[0, A, :])
     put_turned(0, A, 0, tail[...])
-    advance((1, "first", 0))
-
-    @pl.loop(0, 2)
+    x_first, y_first = range(0, tiles + 1, 2), range(1, tiles + 1, 2)
+    advance(1, "first", x_first)
+
+    @unrolled(0, 2)
     def _(n):
         r, landed = half_copy(q2, q2r, 3, 1 - n, prv)
         pl.when(has_next)(landed.wait_recv)
@@ -368,28 +358,32 @@
         q1[r, :] = back(0, r, 0)
 
     pl.when(has_prev)(q1_copy.start)
-
-    @pl.loop(0, 2)
-    def _(n):
-        r = pl.ds(pl.multiple_of(n * half, half), half)
+    advance(1, "first", y_first)
+
+    @unrolled(0, 2)
+    def _(n):
+        r = pl.ds(n * half, half)
         put_outer(0, r, 0, c1[r, :])
 
     gradients(0)
-    advance((0, "first", 0))
-    advance((1, "second", 0))
-
-    @pl.loop(0, 2)
-    def _(n):
-        r = pl.ds(pl.multiple_of(n * half, half), half)
+    advance(0, "first")
+    advance(1, "second", x_first)
+
+    @unrolled(0, 2)
+    def _(n):
+        r = pl.ds(n * half, half)
         c1[r, :] += back(0, r, chan)
 
     ig[0, A, :] = c1[A, :] + q1[B, :]
     pl.when(has_next)(q1_copy.wait_recv)
     ig[0, B, :] = c1[B, :] + q1r[...]
-    advance((1, "z", 0), (0, "second", 0), (1, "relay", 1), (0, "z", 1), (1, "owner", 2), (0, "relay", 2))
-    advance((0, "owner", 0))
-    advance((0, "end", 0))
-    advance((1, "end", 0))
+    advance(1, "second", y_first)
+    stages = [(1, "z", 0), (1, "relay", 1), (1, "owner", 2), (1, "end", 3)]
+    stages += [(0, "second", 0), (0, "z", 2), (0, "relay", 3), (0, "owner", 4), (0, "end", 5)]
+    for tick in range(tiles + 6):
+        for l, what, behind in stages:
+            if 0 <= tick - behind <= tiles:
+                advance(l, what, (tick - behind,))
     if fused:
         for n in range(n_conv):
             conv_o[:, n * TILE:(n + 1) * TILE] = sums[n]

time: 98.4 us -> 112 us (1.14)
  Pallas kernels: 97.6 us -> 111 us
    pallas_call x1, Pallas kernels: 95.6 us -> 110 us  [local(): pl.pallas_call(functools.partial(kernel, n_seq, n_dp, fused, factor), out...]
where the time goes in v6:
time: 112 us
  Pallas kernels  111 us (99%)
    pallas_call x1, Pallas kernels, local(): pl.pallas_call(functools.partial(kernel, n_seq, n_dp, fused, factor), out...  110 us

profile of v6, /device:TPU:0, one launch (start us, length us, event | category | flops | bytes accessed | tf_op | source)
XLA Modules:
  0.0 112.1 jit_solution(17757202501350850008)
XLA Ops:
  0.6 109.5 %shard_map.93 = (f32[1,512,256]{2,1,0:T(8,128)}, f32[32,1024]{1,0:T(8,128)}, f32[32,512]{1,0:T(8,128)}, f32[8,128]{1,0:T(8,128)}) custom-call(f32[1,512,256]{2,1,0:T(8,128)} %refs_0_.1, f32[1,512,256]{2,1,0:T(8,128)} %refs_1_.1, f32[1,512,256]{2,1,0:T(8,128)} %refs_2_.1, f32[2,512,1024]{2,1,0:T(8,128)} %refs_3_.1, f32[2,1024]{1,0:T(2,128)} %refs_4_.1, ...), custom_call_target="tpu_custom_call" | custom-call | tf_op jit(solution)/shard_map/pallas_call | solution.py:439
  110.2 2.0 %shard_map.94 = (f32[1,512,256]{2,1,0:T(8,128)}, f32[32,1024]{1,0:T(8,128)}, f32[32,512]{1,0:T(8,128)}, f32[64]{0:T(128)}) custom-call(f32[1,512,256]{2,1,0:T(8,128)} %get-tuple-element.8.a, f32[32,1024]{1,0:T(8,128)} %get-tuple-element.9.b, f32[32,512]{1,0:T(8,128)} %get-tuple-element.10.c, f32[8,128]{1,0:T(8,128)} %get-tuple-element.11.bias), custom_call_target="tpu_custom_call" | custom-call | tf_op jit(solution)/shard_map/pallas_call | solution.py:450

commit v7 on v5

--- a/solution.py
+++ b/solution.py
@@ -13,6 +13,14 @@
 TILE = 256
 
 
+def unrolled(start, stop):
+    return lambda body: [body(n) for n in range(start, stop)]
+
+
+def aligned(value, size):
+    return value if isinstance(value, int) else pl.multiple_of(value, size)
+
+
 def split(value):
     high = value.astype(BF16)
     return high, (value - high.astype(F32)).astype(BF16)
@@ -84,7 +92,7 @@
     def tiled(extent, body, size=TILE):
         @pl.loop(0, extent // size)
         def _(n):
-            body(pl.ds(pl.multiple_of(n * size, size), size))
+            body(pl.ds(aligned(n * size, size), size))
 
     def split_conv(l):
         fetches["cw%d" % l].wait()
@@ -123,11 +131,11 @@
         oth[l, cols, r], otl[l, cols, r] = split(value.T)
 
     def forward(l, r):
-        @pl.loop(0, gate // TILE)
+        @unrolled(0, gate // TILE)
         def _(n):
             joined = (jh[l, r, :], jl[l, r, :])
-            cols = pl.ds(pl.multiple_of(n * TILE, TILE), TILE)
-            gcols = pl.ds(pl.multiple_of(gate + n * TILE, TILE), TILE)
+            cols = pl.ds(aligned(n * TILE, TILE), TILE)
+            gcols = pl.ds(aligned(gate + n * TILE, TILE), TILE)
             f = dot3(joined, (wch[l, :, cols], wcl[l, :, cols]), NN) + cb[l:l + 1, cols]
             g = dot3(joined, (wch[l, :, gcols], wcl[l, :, gcols]), NN) + cb[l:l + 1, gcols]
             t, s = jnp.tanh(f), jax.nn.sigmoid(g)
@@ -143,10 +151,10 @@
         return value
 
     def dmixed(l, r):
-        @pl.loop(0, gate // TILE)
+        @unrolled(0, gate // TILE)
         def _(n):
-            cols = pl.ds(pl.multiple_of(n * TILE, TILE), TILE)
-            gcols = pl.ds(pl.multiple_of(gate + n * TILE, TILE), TILE)
+            cols = pl.ds(aligned(n * TILE, TILE), TILE)
+            gcols = pl.ds(aligned(gate + n * TILE, TILE), TILE)
             dh = dhs[l, r, cols]
             for part, where in ((dh * fa[l, r, cols], cols), (dh * ga[l, r, cols], gcols)):
                 dzh[l, r, where], dzl[l, r, where] = split(part)
@@ -162,7 +170,7 @@
 
     def put_grad(l, kind, n, value):
         if not fused:
-            (conv_o if kind == 0 else out_o)[l, :, pl.ds(pl.multiple_of(n * TILE, TILE), TILE)] = value
+            (conv_o if kind == 0 else out_o)[l, :, pl.ds(aligned(n * TILE, TILE), TILE)] = value
             return
         block = value.shape[0] // 16
         for j in range(16):
@@ -171,13 +179,13 @@
     def gradients(l):
         @pl.loop(0, n_out)
         def _(n):
-            cols = pl.ds(pl.multiple_of(n * TILE, TILE), TILE)
+            cols = pl.ds(aligned(n * TILE, TILE), TILE)
             put_grad(l, 1, n, dot3((oth[l], otl[l]), (hh[l, :, cols], hl[l, :, cols]), NN))
             step(l, n_conv + n, 0, "core")
 
         @pl.loop(0, n_conv)
         def _(n):
-            cols = pl.ds(pl.multiple_of(n * TILE, TILE), TILE)
+            cols = pl.ds(aligned(n * TILE, TILE), TILE)
             put_grad(l, 0, n, dot3((jth[l], jtl[l]), (dzh[l, :, cols], dzl[l, :, cols]), NN))
             step(l, n, 0, "core")
 
@@ -321,10 +329,10 @@
         split(c2[0]), (woth[1, early, :], wotl[1, early, :]), NN)
     turn_conv(1)
     def half_copy(src, dst, base, i, peer):
-        r = pl.ds(pl.multiple_of(i * half, half), half)
+        r = pl.ds(aligned(i * half, half), half)
         return r, remote(src.at[r], dst.at[r], base + i, base + i, peer, dp)
 
-    @pl.loop(0, 2)
+    @unrolled(0, 2)
     def _(n):
         r, landed = half_copy(x2, x2p, 1, 1 - n, nxt)
         pl.when(has_prev)(landed.wait_recv)
@@ -335,9 +343,9 @@
         _, leaving = half_copy(q2, q2r, 3, 1 - n, prv)
         pl.when(has_prev)(leaving.start)
 
-    @pl.loop(0, 2)
-    def _(n):
-        r = pl.ds(pl.multiple_of(n * half, half), half)
+    @unrolled(0, 2)
+    def _(n):
+        r = pl.ds(aligned(n * half, half), half)
         for l in range(2):
             put_outer(l, r, chan, sk[0, r, :])
         put_outer(1, r, 0, c2[0, r, :])
@@ -346,9 +354,9 @@
 
     gradients(1)
 
-    @pl.loop(0, 2)
-    def _(n):
-        r = pl.ds(pl.multiple_of(n * half, half), half)
+    @unrolled(0, 2)
+    def _(n):
+        r = pl.ds(aligned(n * half, half), half)
         c1[r, :] = c2[0, r, :] + back(1, r, chan)
         put_turned(0, r, chan, x[0, r, :])
 
@@ -357,7 +365,7 @@
     put_turned(0, A, 0, tail[...])
     advance((1, "first", 0))
 
-    @pl.loop(0, 2)
+    @unrolled(0, 2)
     def _(n):
         r, landed = half_copy(q2, q2r, 3, 1 - n, prv)
         pl.when(has_next)(landed.wait_recv)
@@ -369,18 +377,18 @@
 
     pl.when(has_prev)(q1_copy.start)
 
-    @pl.loop(0, 2)
-    def _(n):
-        r = pl.ds(pl.multiple_of(n * half, half), half)
+    @unrolled(0, 2)
+    def _(n):
+        r = pl.ds(aligned(n * half, half), half)
         put_outer(0, r, 0, c1[r, :])
 
     gradients(0)
     advance((0, "first", 0))
     advance((1, "second", 0))
 
-    @pl.loop(0, 2)
-    def _(n):
-        r = pl.ds(pl.multiple_of(n * half, half), half)
+    @unrolled(0, 2)
+    def _(n):
+        r = pl.ds(aligned(n * half, half), half)
         c1[r, :] += back(0, r, chan)
 
     ig[0, A, :] = c1[A, :] + q1[B, :]

time: 98.4 us -> 98.2 us (level)
  no operation moved by 1% of the time
where the time goes in v7:
time: 98.2 us; the launch traced here: 98.1 us
  Pallas kernels  97.4 us (99%)
    pallas_call x1, Pallas kernels, local(): pl.pallas_call(functools.partial(kernel, n_seq, n_dp, fused, factor), out...  95.5 us
    pallas_call x1, Pallas kernels, local(): pl.pallas_call(hand_on, out_shape=[sds(inputs.shape, F32), *grads[:2], sd...  1.98 us

profile of v7, /device:TPU:0, one launch (start us, length us, event | category | flops | bytes accessed | tf_op | source)
XLA Modules:
  0.0 98.1 jit_solution(15163703358114305556)
XLA Ops:
  0.6 95.5 %shard_map.93 = (f32[1,512,256]{2,1,0:T(8,128)}, f32[32,1024]{1,0:T(8,128)}, f32[32,512]{1,0:T(8,128)}, f32[8,128]{1,0:T(8,128)}) custom-call(f32[1,512,256]{2,1,0:T(8,128)} %refs_0_.1, f32[1,512,256]{2,1,0:T(8,128)} %refs_1_.1, f32[1,512,256]{2,1,0:T(8,128)} %refs_2_.1, f32[2,512,1024]{2,1,0:T(8,128)} %refs_3_.1, f32[2,1024]{1,0:T(2,128)} %refs_4_.1, ...), custom_call_target="tpu_custom_call" | custom-call | tf_op jit(solution)/shard_map/pallas_call | solution.py:453
  96.1 2.0 %shard_map.94 = (f32[1,512,256]{2,1,0:T(8,128)}, f32[32,1024]{1,0:T(8,128)}, f32[32,512]{1,0:T(8,128)}, f32[64]{0:T(128)}) custom-call(f32[1,512,256]{2,1,0:T(8,128)} %get-tuple-element.8.a, f32[32,1024]{1,0:T(8,128)} %get-tuple-element.9.b, f32[32,512]{1,0:T(8,128)} %get-tuple-element.10.c, f32[8,128]{1,0:T(8,128)} %get-tuple-element.11.bias), custom_call_target="tpu_custom_call" | custom-call | tf_op jit(solution)/shard_map/pallas_call | solution.py:464
